TPU v7x, 32 devices: a whole 2x2x4 slice. The times are simulated.
32 devices in a mesh: groups: 2 (over x), seq: 16 (over z, y, core).
Axes of the slice: x: 2, y: 2, z: 4, core: 2. Of those that a mesh axis runs over, the one named last changes fastest.
Arguments:
- frames: bfloat16 [16384, 1024], P(('groups', 'seq')), parts along dimension 0, may hold values from -6 to 6
- context: bfloat16 [3072, 512], P(('groups', 'seq')), parts along dimension 0, may hold values from -6 to 6
- noise_level: int32 [128], P(('groups', 'seq')), parts along dimension 0, may hold values from 0 to 7
- alignment: int32 [128, 2], P(('groups', 'seq')), parts along dimension 0, may hold values from 0 to 31, as said below
- counts: int32 [128], P(('groups', 'seq')), parts along dimension 0, may hold values from 1 to 2
- band_width: int32 [16], replicated, may hold values from 0 to 2, as said below
- mod_table: float32 [8, 2048], replicated, may hold values from -3 to 3
- qkv_weight: bfloat16 [1024, 3072], replicated, may hold values from -0.1875 to 0.1875
- out_weight: bfloat16 [1024, 1024], replicated, may hold values from -0.1875 to 0.1875
- cross_query_weight: bfloat16 [1024, 512], replicated, may hold values from -0.1875 to 0.1875
- cross_kv_weight: bfloat16 [512, 1024], replicated, may hold values from -0.25 to 0.25
- cross_out_weight: bfloat16 [512, 1024], replicated, may hold values from -0.25 to 0.25
- banded_attender_factor: float32 [16], replicated, may hold values from 0.5 to 80
- cross_temp: float32 [8], replicated, may hold values from 0.5 to 80
Outputs:
- update: bfloat16 [16384, 1024], P(('groups', 'seq')), parts along dimension 0
There are 2 independent parts, one for each index of `groups`. A program takes and returns all parts, laid end to end along the dimension named above; an argument that names none is the same for every part. Nothing has to cross between parts.
Inputs may be any that keep to these rules, and one draw needn't show every extreme that they name: `alignment`: the entries of each list are distinct consecutive token blocks, all within 1 token blocks of (b * 2) // 4 for frame block b. Among the rows of one device, the list of the first frame block starts as low as that allows and the list of the last frame block ends as high as that allows and has all slots live, both within the excerpt's token blocks. `band_width`: some head has band width 2.
All inputs are finite; a program needn't handle non-finite values.
Results may differ from a plain program's by a relative error of at most 0.0045.
The roundings to bfloat16 on the way count: a program that leaves them out, or rounds other values in their place, can miss the bound.
Values may be sent and summed in bfloat16 or wider, within the bound.
No kernel may reach another device: no remote copies, remote signals or barrier semaphores. Data moves between devices by JAX's collectives and lax.ppermute only.
A program may use at most 192 MiB of HBM per device.

v0:
```python
import jax
import jax.numpy as jnp
from jax import lax
from jax.sharding import PartitionSpec as P

BANDED_ATTEND_CT = 16
MIXED_ATTEND_CNT = 8
HD = 64
LEVELS = 8
BLK = 128
WMAX = 2
TOKB = 48
RCH = 1
ALIST = 2


def with_halo(block, sides, width):
    for axis, dim in sides:
        count = lax.axis_size(axis)
        forward = [(i, i + 1) for i in range(count - 1)]
        backward = [(target, source) for source, target in forward]
        low = lax.ppermute(
            lax.slice_in_dim(block, block.shape[dim] - width, None, axis=dim), axis, forward
        )
        high = lax.ppermute(lax.slice_in_dim(block, 0, width, axis=dim), axis, backward)
        block = jnp.concatenate([low, block, high], axis=dim)
    return block


def head_norm(matrix, heads):
    count_rows = matrix.shape[0]
    parts = matrix.reshape(count_rows, heads, -1)
    parts = parts * lax.rsqrt(jnp.mean(parts * parts, axis=-1, keepdims=True) + 1e-06)
    return parts.reshape(count_rows, -1)


def masked_softmax(scores, allowed):
    scores = jnp.where(allowed, scores, -jnp.inf)
    peak = jnp.max(scores, axis=-1, keepdims=True)
    powers = jnp.exp(scores - peak)
    return powers / jnp.sum(powers, axis=-1, keepdims=True)


def shards(
    frames,
    context,
    noise_level,
    alignment,
    counts,
    band_width,
    mod_table,
    qkv_weight,
    out_weight,
    cross_query_weight,
    cross_kv_weight,
    cross_out_weight,
    banded_attender_factor,
    cross_temp,
):
    frame_rows, model_width = frames.shape
    query_width = qkv_weight.shape[1] // 3
    cross_width = cross_query_weight.shape[1]
    devices = lax.axis_size("seq")
    device = lax.axis_index("seq")
    local_blocks = frame_rows // BLK
    total_blocks = local_blocks * devices
    input_arrays = frames.astype(jnp.float32)
    normed = input_arrays * lax.rsqrt(
        jnp.mean(input_arrays * input_arrays, axis=1, keepdims=True) + 1e-06
    )
    onehot = (noise_level[:, None] == jnp.arange(LEVELS, dtype=jnp.int32)[None, :]).astype(
        jnp.float32
    )
    modulation = jnp.dot(onehot, mod_table, precision=lax.Precision.HIGHEST)
    hidden = (
        (
            normed.reshape(local_blocks, BLK, model_width)
            * (1.0 + modulation[:, None, :model_width])
            + modulation[:, None, model_width:]
        )
        .reshape(frame_rows, model_width)
        .astype(jnp.bfloat16)
    )
    alignment_slack = WMAX * BLK
    projected = jnp.dot(hidden, qkv_weight, preferred_element_type=jnp.float32)
    queries = head_norm(projected[:, :query_width], BANDED_ATTEND_CT).astype(jnp.bfloat16)
    local_pairs = jnp.concatenate(
        [
            head_norm(projected[:, query_width : 2 * query_width], BANDED_ATTEND_CT).astype(
                jnp.bfloat16
            ),
            projected[:, 2 * query_width :].astype(jnp.bfloat16),
        ],
        1,
    )
    key_pairs = with_halo(local_pairs, (("seq", 0),), alignment_slack)
    token_rows_local = context.shape[0]
    token_blocks = token_rows_local // TOKB
    cross_margin = RCH * TOKB
    context_pad = with_halo(context, (("seq", 0),), cross_margin)
    cross_proj = jnp.dot(context_pad, cross_kv_weight, preferred_element_type=jnp.float32)
    cross_pairs = jnp.concatenate(
        [
            head_norm(cross_proj[:, :cross_width], MIXED_ATTEND_CNT).astype(jnp.bfloat16),
            cross_proj[:, cross_width:].astype(jnp.bfloat16),
        ],
        1,
    )
    window_tokens = cross_pairs.shape[0]
    cross_keys = cross_pairs[:, :cross_width].reshape(window_tokens, MIXED_ATTEND_CNT, HD)
    cross_values = cross_pairs[:, cross_width:].reshape(window_tokens, MIXED_ATTEND_CNT, HD)
    token_block = device * token_blocks - RCH + jnp.arange(window_tokens, dtype=jnp.int32) // TOKB
    live_slots = jnp.arange(ALIST, dtype=jnp.int32)[None, :] < counts[:, None]
    block_allowed = jnp.any(
        (alignment[:, :, None] == token_block[None, None, :]) & live_slots[:, :, None], axis=1
    )
    cross_queries = head_norm(
        jnp.dot(hidden, cross_query_weight, preferred_element_type=jnp.float32), MIXED_ATTEND_CNT
    ).astype(jnp.bfloat16)
    self_scale = banded_attender_factor * HD ** (-0.5)
    cross_scale = cross_temp * HD ** (-0.5)
    group_rows = min(frame_rows, 512)
    group_count = frame_rows // group_rows
    group_blocks = group_rows // BLK

    def attend(group):
        first_row = group * group_rows
        query_rows = queries.reshape(group_rows, BANDED_ATTEND_CT, HD)
        key_rows = key_pairs[:, :query_width].reshape(-1, BANDED_ATTEND_CT, HD)
        value_rows = key_pairs[:, query_width:].reshape(-1, BANDED_ATTEND_CT, HD)
        query_block = (
            device * local_blocks + (first_row + jnp.arange(group_rows, dtype=jnp.int32)) // BLK
        )
        key_block = (
            device * local_blocks
            - WMAX
            + (first_row + jnp.arange(group_rows + 2 * alignment_slack, dtype=jnp.int32)) // BLK
        )
        within_band_flag = (
            jnp.abs(query_block[:, None] - key_block[None, :])[None, :, :]
            <= band_width[:, None, None]
        ) & ((key_block >= 0) & (key_block < total_blocks))[None, None, :]
        scores = (
            jnp.einsum("ihd,jhd->hij", query_rows, key_rows, preferred_element_type=jnp.float32)
            * self_scale[:, None, None]
        )
        weights = masked_softmax(scores, within_band_flag).astype(jnp.bfloat16)
        self_out = (
            jnp.einsum("hij,jhd->ihd", weights, value_rows, preferred_element_type=jnp.float32)
            .reshape(group_rows, query_width)
            .astype(jnp.bfloat16)
        )
        cross_rows = cross_queries.reshape(group_rows, MIXED_ATTEND_CNT, HD)
        row_allowed = jnp.broadcast_to(
            block_allowed[:, None, :], (group_blocks, BLK, window_tokens)
        ).reshape(group_rows, window_tokens)
        cross_scores = (
            jnp.einsum("ihd,jhd->hij", cross_rows, cross_keys, preferred_element_type=jnp.float32)
            * cross_scale[:, None, None]
        )
        cross_weights = masked_softmax(cross_scores, row_allowed[None, :, :]).astype(jnp.bfloat16)
        cross_out = (
            jnp.einsum(
                "hij,jhd->ihd", cross_weights, cross_values, preferred_element_type=jnp.float32
            )
            .reshape(group_rows, cross_width)
            .astype(jnp.bfloat16)
        )
        total = jnp.dot(self_out, out_weight, preferred_element_type=jnp.float32) + jnp.dot(
            cross_out, cross_out_weight, preferred_element_type=jnp.float32
        )
        return total.astype(jnp.bfloat16)

    result = lax.map(attend, jnp.arange(group_count, dtype=jnp.int32))
    return result.reshape(frame_rows, model_width)


def solution(mesh):
    placed = (
        P(("groups", "seq"), None),
        P(("groups", "seq"), None),
        P(("groups", "seq")),
        P(("groups", "seq"), None),
        P(("groups", "seq")),
        P(),
        P(),
        P(),
        P(),
        P(),
        P(),
        P(),
        P(),
        P(),
    )
    return jax.shard_map(
        shards, mesh=mesh, in_specs=placed, out_specs=P(("groups", "seq"), None), check_vma=False
    )
```

profile of v0, /device:TPU:1, one launch (start us, length us, event | category | flops | bytes accessed | tf_op | source)
XLA Modules:
  0.0 132.4 jit_solution(831613482611971934)
XLA Ops:
  0.0 1.0 fusion.46
  1.0 4.7 %collective-permute-start.2 = (bf16[48,512]{1,0:T(8,128)(2,1)S(1)}, bf16[48,512]{1,0:T(8,128)(2,1)S(1)}, u32[]{:S(2)}, u32[]{:S(2)}) collective-permute-start(bf16[48,512]{1,0:T(8,128)(2,1)S(1)} %get-tuple-element.39), channel_id=1, source_target_pairs={{0,1},{1,2},{2,3},{3,4},{4,5},{5,6},{6,7},{7,8},{8,9},{9,10},{10,1... | collective-permute-start | bytes 147464 | tf_op jit(solution)/shard_map/ppermute | solution.py:22
  5.7 1.9 %collective-permute-start.3 = (bf16[48,512]{1,0:T(8,128)(2,1)S(1)}, bf16[48,512]{1,0:T(8,128)(2,1)S(1)}, u32[]{:S(2)}, u32[]{:S(2)}) collective-permute-start(bf16[48,512]{1,0:T(8,128)(2,1)S(1)} %get-tuple-element.40), channel_id=1, source_target_pairs={{1,0},{2,1},{3,2},{4,3},{5,4},{6,5},{7,6},{8,7},{9,8},{10,9},{11,1... | collective-permute-start | bytes 147464 | tf_op jit(solution)/shard_map/ppermute | solution.py:25
  7.6 1.5 %fusion.10 = f32[512]{0:T(512)S(1)} fusion(bf16[512,1024]{1,0:T(8,128)(2,1)} %param.14), kind=kLoop, calls=%fused_computation.19 | loop fusion | flops 1572352 | bytes 1050624 | tf_op jit(solution)/shard_map/reduce_sum | solution.py:69
  9.1 1.1 fusion.39
  10.2 0.4 fusion.13
  10.6 0.0 copy-start.6
  10.6 5.9 %fusion.51 = f32[512,3072]{1,0:T(8,128)S(1)} fusion(bf16[512,1024]{1,0:T(8,128)(2,1)S(1)} %fusion.13, bf16[1024,3072]{1,0:T(8,128)(2,1)} %param.21), kind=kOutput, calls=%fused_computation.102 | convolution fusion | flops 3221225472 | bytes 13631488 | tf_op jit(solution)/shard_map/dot_general | solution.py:85
  16.5 1.4 %slice.82 = bf16[512,1024]{1,0:T(8,128)(2,1)} slice(f32[512,3072]{1,0:T(8,128)S(1)} %fusion.51), slice={[0:512], [2048:3072]} | slice | bytes 2097152 | tf_op jit(solution)/shard_map/slice | solution.py:92
  17.9 2.9 %slice_multiply_fusion = (f32[512,1024]{1,0:T(8,128)}, f32[512,1024]{1,0:T(8,128)}) fusion(f32[512,3072]{1,0:T(8,128)S(1)} %fusion.51), kind=kLoop, calls=%fused_computation.32 | loop fusion | flops 1048576 | bytes 8388608 | tf_op jit(solution)/shard_map/mul | solution.py:33
  20.8 2.9 %copy.38 = f32[512,1024]{0,1:T(8,128)} copy(f32[512,1024]{1,0:T(8,128)} %get-tuple-element.33) | data formatting | bytes 4194304 | tf_op jit(solution)/shard_map/mul | solution.py:33
  23.7 1.9 %bitcast_reduce_fusion = f32[512,16]{0,1:T(8,128)S(1)} fusion(f32[512,1024]{0,1:T(8,128)} %copy.38), kind=kLoop, calls=%fused_computation.26 | loop fusion | flops 516096 | bytes 2129920 | tf_op jit(solution)/shard_map/reduce_sum | solution.py:33
  25.6 1.6 %mul.138 = f32[512,16,64]{0,2,1:T(8,128)} broadcast(f32[512,16]{0,1:T(8,128)S(1)} %add_rsqrt_fusion), dimensions={0,1} | broadcast | bytes 2129920 | tf_op jit(solution)/shard_map/mul | solution.py:33
  27.2 2.9 %copy.39 = f32[512,1024]{1,0:T(8,128)} copy(f32[512,1024]{0,1:T(8,128)} %bitcast.54) | data formatting | bytes 4194304 | tf_op jit(solution)/shard_map/mul | solution.py:33
  30.1 2.9 %copy.35 = f32[512,1024]{0,1:T(8,128)} copy(f32[512,1024]{1,0:T(8,128)} %get-tuple-element.34) | data formatting | bytes 4194304 | tf_op jit(solution)/shard_map/mul | solution.py:33
  33.0 1.9 %bitcast_reduce_fusion.1 = f32[512,16]{0,1:T(8,128)S(1)} fusion(f32[512,1024]{0,1:T(8,128)} %copy.35), kind=kLoop, calls=%fused_computation.27 | loop fusion | flops 516096 | bytes 2129920 | tf_op jit(solution)/shard_map/reduce_sum | solution.py:33
  34.9 1.6 %mul.132 = f32[512,16,64]{0,2,1:T(8,128)} broadcast(f32[512,16]{0,1:T(8,128)S(1)} %add_rsqrt_fusion.1), dimensions={0,1} | broadcast | bytes 2129920 | tf_op jit(solution)/shard_map/mul | solution.py:33
  36.4 2.9 %copy.36 = f32[512,1024]{1,0:T(8,128)} copy(f32[512,1024]{0,1:T(8,128)} %bitcast.55) | data formatting | bytes 4194304 | tf_op jit(solution)/shard_map/mul | solution.py:33
  39.3 5.2 %multiply_convert_fusion = (bf16[512,1024]{1,0:T(8,128)(2,1)}, bf16[512,1024]{1,0:T(8,128)(2,1)S(1)}) fusion(f32[512,1024]{1,0:T(8,128)} %copy.39, f32[512,3072]{1,0:T(8,128)} %copy-done.1, f32[512,1024]{1,0:T(8,128)} %copy.36), kind=kLoop, calls=%fused_computation.29 | loop fusion | flops 2097152 | bytes 10485760 | tf_op jit(solution)/shard_map/convert_element_type | solution.py:86
  44.6 0.0 copy-start.16
  44.6 1.5 %fusion.20 = (bf16[256,2048]{1,0:T(8,128)(2,1)}, bf16[256,2048]{1,0:T(8,128)(2,1)}) fusion(bf16[512,1024]{1,0:T(8,128)(2,1)S(1)} %get-tuple-element.32, bf16[512,1024]{1,0:T(8,128)(2,1)S(1)} %copy-done.2), kind=kLoop, calls=%fused_computation.40 | loop fusion | flops 4194304 | bytes 4194304 | tf_op jit(solution)/shard_map/concatenate | solution.py:87
  46.1 3.6 %collective-permute-start = (bf16[256,2048]{1,0:T(8,128)(2,1)}, bf16[256,2048]{1,0:T(8,128)(2,1)}, u32[]{:S(2)}, u32[]{:S(2)}) collective-permute-start(bf16[256,2048]{1,0:T(8,128)(2,1)} %get-tuple-element.37), channel_id=1, source_target_pairs={{0,1},{1,2},{2,3},{3,4},{4,5},{5,6},{6,7},{7,8},{8,9},{9,10},{10,1... | collective-permute-start | bytes 3145736 | tf_op jit(solution)/shard_map/ppermute | solution.py:22
  49.7 2.1 %collective-permute-start.1 = (bf16[256,2048]{1,0:T(8,128)(2,1)}, bf16[256,2048]{1,0:T(8,128)(2,1)}, u32[]{:S(2)}, u32[]{:S(2)}) collective-permute-start(bf16[256,2048]{1,0:T(8,128)(2,1)} %get-tuple-element.38), channel_id=1, source_target_pairs={{1,0},{2,1},{3,2},{4,3},{5,4},{6,5},{7,6},{8,7},{9,8},{10,9},{11,1... | collective-permute-start | bytes 3145736 | tf_op jit(solution)/shard_map/ppermute | solution.py:25
  51.9 0.6 broadcast_multiply_fusion.1
  52.5 0.6 broadcast_multiply_fusion
  53.1 2.3 %copy.44 = bf16[1024,512]{0,1:T(8,128)(2,1)} copy(bf16[1024,512]{1,0:T(8,128)(2,1)} %param.23) | data formatting | bytes 2097152 | tf_op args[9]
  55.4 3.3 %multiply_reduce_fusion = (f32[512,8]{0,1:T(8,128)S(1)}, f32[512,8,64]{0,2,1:T(8,128)}) fusion(bf16[8,64,1024]{2,1,0:T(8,128)(2,1)} %bitcast.62, bf16[512,1024]{1,0:T(8,128)(2,1)} %copy-done.6), kind=kOutput, calls=%fused_computation.45 | convolution fusion | flops 537391104 | bytes 3162112 | tf_op jit(solution)/shard_map/dot_general | solution.py:118
  58.7 0.0 copy-start.10
  58.7 1.7 %subtract_abs_fusion = s32[512,1024]{1,0:T(8,128)} fusion(s32[1024]{0:T(1024)S(1)} %fusion.31, s32[512]{0:T(512)S(1)} %fusion.35), kind=kLoop, calls=%fused_computation.30 | loop fusion | flops 1048576 | bytes 2103296 | tf_op jit(solution)/shard_map/while/body/eval_jaxpr/abs | solution.py:140
  60.4 0.1 and_reduce_fusion
  60.4 0.6 compare_and_fusion
  61.0 0.2 copy.43
  61.2 0.3 broadcast_in_dim.74
  61.5 0.7 copy.50
  62.1 2.3 %copy.40 = bf16[512,1024]{0,1:T(8,128)(2,1)} copy(bf16[512,1024]{1,0:T(8,128)(2,1)} %get-tuple-element.31) | data formatting | bytes 2097152 | tf_op jit(solution)/shard_map/convert_element_type | solution.py:86
  64.4 0.0 collective-permute-done.2
  64.4 0.0 collective-permute-done.3
  64.4 1.6 %fusion.25 = f32[192,1024]{1,0:T(8,128)S(1)} fusion(bf16[512,1024]{1,0:T(8,128)(2,1)} %param.24, bf16[48,512]{1,0:T(8,128)(2,1)S(1)} %collective-permute-done.3, bf16[96,512]{1,0:T(8,128)(2,1)S(1)} %copy-done.10, bf16[48,512]{1,0:T(8,128)(2,1)S(1)} %collective-permute-done.2), kind=kOutput, calls=%fused_computation.53 | convolution fusion | flops 201916416 | bytes 2031616 | tf_op jit(solution)/shard_map/dot_general | solution.py:101
  66.1 0.0 copy-start.5
  66.1 0.8 slice.83
  66.8 0.1 copy-done.5
  67.0 1.8 %copy.42 = bf16[192,512]{0,1:T(8,128)(2,1)} copy(bf16[192,512]{1,0:T(8,128)(2,1)} %slice.83) | data formatting | bytes 393216 | tf_op jit(solution)/shard_map/slice | solution.py:105
  68.8 1.0 copy.45
  69.8 1.1 bitcast_reduce_fusion.2
  70.9 0.9 mul.150
  71.8 1.2 copy.46
  73.0 1.7 %multiply_convert_fusion.4 = bf16[192,512]{1,0:T(8,128)(2,1)} fusion(f32[192,512]{1,0:T(8,128)S(1)} %copy.46, f32[192,1024]{1,0:T(8,128)} %copy-done.5), kind=kLoop, calls=%fused_computation.50 | loop fusion | flops 196608 | bytes 983040 | tf_op jit(solution)/shard_map/convert_element_type | solution.py:104
  74.8 1.1 copy.47
  75.8 1.9 %fusion.23 = f32[8,512,192]{1,2,0:T(8,128)S(1)} fusion(bf16[192,8,64]{0,2,1:T(8,128)(2,1)S(1)} %bitcast.60, f32[512,8,64]{0,2,1:T(8,128)} %get-tuple-element.62, f32[512,8]{0,1:T(8,128)S(1)} %add_rsqrt_fusion.2), kind=kOutput, calls=%fused_computation.46 | convolution fusion | flops 101187584 | bytes 4407296 | tf_op jit(solution)/shard_map/while/body/eval_jaxpr/ihd,jhd->hij/dot_general | solution.py:158
  77.7 1.4 %fusion.48 = (f32[8,512]{1,0:T(8,128)S(1)}, f32[8,512,192]{1,2,0:T(8,128)S(1)}) fusion(f32[8,512,192]{1,2,0:T(8,128)S(1)} %fusion.23, f32[8]{0:T(128)S(1)} %copy-done.20, pred[512,192]{0,1:T(8,128)(4,1)S(1)} %bitcast.66), kind=kOutput, calls=%fused_computation.100 | output fusion | flops 4718783 | bytes 6406176 | tf_op jit(solution)/shard_map/while/body/eval_jaxpr/sub | solution.py:40
  79.2 1.2 fusion.19
  80.5 0.0 collective-permute-done
  80.5 0.0 collective-permute-done.1
  80.5 2.7 %pad_maximum_fusion = bf16[1024,2048]{1,0:T(8,128)(2,1)S(1)} fusion(bf16[256,2048]{1,0:T(8,128)(2,1)} %collective-permute-done.1, bf16[512,1024]{1,0:T(8,128)(2,1)S(1)} %copy-done.3, bf16[512,1024]{1,0:T(8,128)(2,1)S(1)} %get-tuple-element.32, bf16[256,2048]{1,0:T(8,128)(2,1)} %collective-permute-done), kind=kLoop, calls=%fused_computation.12 | loop fusion | flops 16777216 | bytes 8388608 | tf_op jit(solution)/shard_map/concatenate | solution.py:26
  83.2 2.4 %fusion.45 = (bf16[1024,1024]{1,0:T(8,128)(2,1)}, bf16[1024,1024]{1,0:T(8,128)(2,1)}) fusion(bf16[1024,2048]{1,0:T(8,128)(2,1)S(1)} %pad_maximum_fusion), kind=kLoop, calls=%fused_computation.97 | loop fusion | bytes 8388608 | tf_op jit(solution)/shard_map/while/body/eval_jaxpr/slice | solution.py:129
  85.6 4.0 %copy.41 = bf16[1024,1024]{0,1:T(8,128)(2,1)} copy(bf16[1024,1024]{1,0:T(8,128)(2,1)} %get-tuple-element.35) | data formatting | bytes 4194304 | tf_op jit(solution)/shard_map/while/body/eval_jaxpr/slice | solution.py:129
  89.6 4.0 %copy.37 = bf16[1024,1024]{0,1:T(8,128)(2,1)} copy(bf16[1024,1024]{1,0:T(8,128)(2,1)} %get-tuple-element.36) | data formatting | bytes 4194304 | tf_op jit(solution)/shard_map/while/body/eval_jaxpr/slice | solution.py:130
  93.6 21.8 %fusion.47 = (f32[16,512]{1,0:T(8,128)S(1)}, f32[16,512,1024]{2,1,0:T(8,128)}) fusion(f32[16]{0:T(128)S(1)} %copy-done.19, s32[512,1024]{1,0:T(8,128)} %subtract_abs_fusion, s32[16]{0:T(128)S(1)} %copy-done.17, pred[1024]{0:T(1024)(128)(4,1)S(1)} %copy-done.18, bf16[512,16,64]{0,2,1:T(8,128)(2,1)S(1)} %bitcast.61, bf16[1024,16,64]{0,2,1:T(8,128)(2,1)} %bitcast.57), kind=kOutput, calls=%fused_computation.99 | convolution fusion | flops 1124074496 | bytes 38831232 | tf_op jit(solution)/shard_map/while/body/eval_jaxpr/sub | solution.py:40
  115.4 13.9 %fusion.18 = bf16[16,64,512]{2,1,0:T(8,128)(2,1)S(1)} fusion(bf16[1024,16,64]{0,2,1:T(8,128)(2,1)} %bitcast.58, f32[16,512,1024]{2,1,0:T(8,128)} %get-tuple-element.60, f32[16,512]{1,0:T(8,128)S(1)} %get-tuple-element.58), kind=kOutput, calls=%fused_computation.38 | convolution fusion | flops 1091043328 | bytes 36732928 | tf_op jit(solution)/shard_map/while/body/eval_jaxpr/hij,jhd->ihd/dot_general | solution.py:149
  129.4 0.0 copy-start.8
  129.4 0.0 copy-start.9
  129.4 1.3 fusion.52
  130.7 0.1 copy-done.9
  130.7 1.7 %add_convert_fusion = bf16[512,1024]{1,0:T(8,128)(2,1)} fusion(f32[512,1024]{1,0:T(8,128)S(1)} %fusion.52, bf16[512,512]{0,1:T(8,128)(2,1)S(1)} %bitcast.63, bf16[512,1024]{1,0:T(8,128)(2,1)S(1)} %copy-done.8), kind=kOutput, calls=%fused_computation.28 | convolution fusion | flops 537919488 | bytes 4718592 | tf_op jit(solution)/shard_map/while/body/eval_jaxpr/dot_general | solution.py:169
  (45 shorter events, 0.2 us)
Async XLA Ops:
  0.0 129.3 %copy-start = (bf16[1024,1024]{1,0:T(8,128)(2,1)S(1)}, bf16[1024,1024]{1,0:T(8,128)(2,1)}, u32[]{:S(2)}) copy-start(bf16[1024,1024]{1,0:T(8,128)(2,1)} %param.22) | copy-start | bytes 6291460
  0.0 10.2 %copy-start.4 = (bf16[512,1024]{1,0:T(8,128)(2,1)S(1)}, bf16[512,1024]{1,0:T(8,128)(2,1)}, u32[]{:S(2)}) copy-start(bf16[512,1024]{1,0:T(8,128)(2,1)} %param.14) | copy-start | bytes 3145732
  1.0 63.4 %collective-permute-start.2 = (bf16[48,512]{1,0:T(8,128)(2,1)S(1)}, bf16[48,512]{1,0:T(8,128)(2,1)S(1)}, u32[]{:S(2)}, u32[]{:S(2)}) collective-permute-start(bf16[48,512]{1,0:T(8,128)(2,1)S(1)} %get-tuple-element.39), channel_id=1, source_target_pairs={{0,1},{1,2},{2,3},{3,4},{4,5},{5,6},{6,7},{7,8},{8,9},{9,10},{10,1... | collective-permute-start | bytes 147464 | tf_op jit(solution)/shard_map/ppermute | solution.py:22
  5.7 58.8 %collective-permute-start.3 = (bf16[48,512]{1,0:T(8,128)(2,1)S(1)}, bf16[48,512]{1,0:T(8,128)(2,1)S(1)}, u32[]{:S(2)}, u32[]{:S(2)}) collective-permute-start(bf16[48,512]{1,0:T(8,128)(2,1)S(1)} %get-tuple-element.40), channel_id=1, source_target_pairs={{1,0},{2,1},{3,2},{4,3},{5,4},{6,5},{7,6},{8,7},{9,8},{10,9},{11,1... | collective-permute-start | bytes 147464 | tf_op jit(solution)/shard_map/ppermute | solution.py:25
  10.6 5.9 %copy-start.6 = (bf16[512,1024]{1,0:T(8,128)(2,1)}, bf16[512,1024]{1,0:T(8,128)(2,1)S(1)}, u32[]{:S(2)}) copy-start(bf16[512,1024]{1,0:T(8,128)(2,1)S(1)} %fusion.13) | copy-start | bytes 3145732
  16.5 4.3 %copy-start.1 = (f32[512,3072]{1,0:T(8,128)}, f32[512,3072]{1,0:T(8,128)S(1)}, u32[]{:S(2)}) copy-start(f32[512,3072]{1,0:T(8,128)S(1)} %fusion.51) | copy-start | bytes 18874372
  39.3 5.3 %copy-start.2 = (bf16[512,1024]{1,0:T(8,128)(2,1)S(1)}, bf16[512,1024]{1,0:T(8,128)(2,1)}, u32[]{:S(2)}) copy-start(bf16[512,1024]{1,0:T(8,128)(2,1)} %slice.82) | copy-start | bytes 3145732
  44.6 7.3 %copy-start.14 = (s32[4]{0:T(128)S(1)}, s32[4]{0:T(128)}, u32[]{:S(2)}) copy-start(s32[4]{0:T(128)} %param.18) | copy-start | bytes 52
  44.6 7.3 %copy-start.15 = (f32[16]{0:T(128)S(1)}, f32[16]{0:T(128)}, u32[]{:S(2)}) copy-start(f32[16]{0:T(128)} %param.26) | copy-start | bytes 196
  44.6 7.9 %copy-start.16 = (f32[8]{0:T(128)S(1)}, f32[8]{0:T(128)}, u32[]{:S(2)}) copy-start(f32[8]{0:T(128)} %param.27) | copy-start | bytes 100
  46.1 34.4 %collective-permute-start = (bf16[256,2048]{1,0:T(8,128)(2,1)}, bf16[256,2048]{1,0:T(8,128)(2,1)}, u32[]{:S(2)}, u32[]{:S(2)}) collective-permute-start(bf16[256,2048]{1,0:T(8,128)(2,1)} %get-tuple-element.37), channel_id=1, source_target_pairs={{0,1},{1,2},{2,3},{3,4},{4,5},{5,6},{6,7},{7,8},{8,9},{9,10},{10,1... | collective-permute-start | bytes 3145736 | tf_op jit(solution)/shard_map/ppermute | solution.py:22
  49.7 30.7 %collective-permute-start.1 = (bf16[256,2048]{1,0:T(8,128)(2,1)}, bf16[256,2048]{1,0:T(8,128)(2,1)}, u32[]{:S(2)}, u32[]{:S(2)}) collective-permute-start(bf16[256,2048]{1,0:T(8,128)(2,1)} %get-tuple-element.38), channel_id=1, source_target_pairs={{1,0},{2,1},{3,2},{4,3},{5,4},{6,5},{7,6},{8,7},{9,8},{10,9},{11,1... | collective-permute-start | bytes 3145736 | tf_op jit(solution)/shard_map/ppermute | solution.py:25
  58.7 1.7 %copy-start.13 = (s32[4,2]{0,1:T(2,128)S(1)}, s32[4,2]{0,1:T(2,128)}, u32[]{:S(2)}) copy-start(s32[4,2]{0,1:T(2,128)} %param.17) | copy-start | bytes 100
  58.7 5.8 %copy-start.10 = (bf16[96,512]{1,0:T(8,128)(2,1)S(1)}, bf16[96,512]{1,0:T(8,128)(2,1)}, u32[]{:S(2)}) copy-start(bf16[96,512]{1,0:T(8,128)(2,1)} %param.15) | copy-start | bytes 294916
  66.1 0.9 copy-start.5
  75.8 1.9 %copy-start.12 = (pred[24,8,4,128]{3,1,2,0:T(8,128)(4,1)S(1)}, pred[24,8,4,128]{3,1,2,0:T(8,128)(4,1)}, u32[]{:S(2)}) copy-start(pred[24,8,4,128]{3,1,2,0:T(8,128)(4,1)} %copy.50) | copy-start | bytes 294916
  75.8 1.9 %copy-start.20 = (f32[8]{0:T(128)S(1)}, f32[8]{0:T(128)}, u32[]{:S(2)}) copy-start(f32[8]{0:T(128)} %broadcast_multiply_fusion) | copy-start | bytes 100
  77.7 1.5 %copy-start.11 = (bf16[192,512]{0,1:T(8,128)(2,1)S(1)}, bf16[192,512]{0,1:T(8,128)(2,1)}, u32[]{:S(2)}) copy-start(bf16[192,512]{0,1:T(8,128)(2,1)} %copy.42) | copy-start | bytes 589828
  79.2 1.3 copy-start.3
  89.6 4.0 %copy-start.7 = (bf16[512,1024]{0,1:T(8,128)(2,1)S(1)}, bf16[512,1024]{0,1:T(8,128)(2,1)}, u32[]{:S(2)}) copy-start(bf16[512,1024]{0,1:T(8,128)(2,1)} %copy.40) | copy-start | bytes 3145732
  89.6 4.0 %copy-start.17 = (s32[16]{0:T(128)S(1)}, s32[16]{0:T(128)}, u32[]{:S(2)}) copy-start(s32[16]{0:T(128)} %param.19) | copy-start | bytes 196
  89.6 4.0 %copy-start.18 = (pred[1024]{0:T(1024)(128)(4,1)S(1)}, pred[1024]{0:T(1024)(128)(4,1)}, u32[]{:S(2)}) copy-start(pred[1024]{0:T(1024)(128)(4,1)} %compare_and_fusion) | copy-start | bytes 3076
  89.6 4.0 %copy-start.19 = (f32[16]{0:T(128)S(1)}, f32[16]{0:T(128)}, u32[]{:S(2)}) copy-start(f32[16]{0:T(128)} %broadcast_multiply_fusion.1) | copy-start | bytes 196
  129.4 1.3 copy-start.8
  129.4 1.3 %copy-start.9 = (bf16[8,64,512]{2,1,0:T(8,128)(2,1)S(1)}, bf16[8,64,512]{2,1,0:T(8,128)(2,1)}, u32[]{:S(2)}) copy-start(bf16[8,64,512]{2,1,0:T(8,128)(2,1)} %fusion.19) | copy-start | bytes 1572868
where the time goes:
time: 134 us; the launch traced here: 132 us
  matrix products  53.7 us (40%)
  local copies, waits for them, and re-layouts  40.2 us (30%)
  other arithmetic  25.8 us (19%)
  starting transfers between devices  12.3 us (9%)
    sub x1, matrix products, masked_softmax(): powers = jnp.exp(scores - peak)  21.8 us
    dot_general x1, matrix products, attend(): jnp.einsum('hij,jhd->ihd', weights, value_rows, preferred_element_type=jn...  13.9 us
    mul x6, local copies, waits for them, and re-layouts, head_norm(): parts * lax.rsqrt(jnp.mean(parts * parts, axis=-1, keepdims=True) + 1e-06)  11 us
    ppermute x2, starting transfers between devices, with_halo(): lax.ppermute(lax.slice_in_dim(block, block.shape[dim] - width, None, axis...  8.29 us
    mul x3, local copies, waits for them, and re-layouts, head_norm(): parts * parts  6.79 us
    slice x2, local copies, waits for them, and re-layouts, attend(): key_rows = key_pairs[:, :query_width].reshape(-1, BANDED_ATTEND_CT, HD)  6.37 us
    dot_general x1, matrix products, shards(): projected = jnp.dot(hidden, qkv_weight, preferred_element_type=jnp.float32)  5.9 us
    convert_element_type x1, other arithmetic, shards(): head_norm(projected[:, :query_width], BANDED_ATTEND_CT).astype(jnp.bfloat16)  5.25 us
  transfers between devices with their start and end apart: 4, of which 0 were waited for; matrix products, arithmetic and copies ran while one was open for 50% of the time, Pallas kernels for 0%

commit v1 on v0

v1 whole, which is shorter than its diff:
```python
import functools

import jax
import jax.numpy as jnp
from jax import lax
from jax.experimental import pallas as pl
from jax.experimental.pallas import tpu as pltpu
from jax.sharding import PartitionSpec as P

BANDED_ATTEND_CT = 16
MIXED_ATTEND_CNT = 8
HD = 64
LEVELS = 8
BLK = 128
WMAX = 2
TOKB = 48
RCH = 1
ALIST = 2

LANES = 128
GROUP = 4
GCOLS = GROUP * HD
LOG2E = 1.4426950408889634
OFF = -1e30
PLAIN_FACTOR = 8.0
F32 = jnp.float32
BF16 = jnp.bfloat16
TOK_PACK = 32


def dot(a, b):
    return jnp.dot(a, b, preferred_element_type=F32)


def dot_t(a, b):
    return lax.dot_general(a, b, (((1,), (1,)), ((), ())), preferred_element_type=F32)


def head_mean(width):
    row = lax.broadcasted_iota(jnp.int32, (width, width), 0) // HD
    col = lax.broadcasted_iota(jnp.int32, (width, width), 1) // HD
    return jnp.where(row == col, 1.0 / HD, 0.0).astype(BF16)


def head_norm(x, mean):
    square = x * x
    high = square.astype(BF16)
    low = (square - high.astype(F32)).astype(BF16)
    ms = dot(high, mean) + dot(low, mean)
    return (x * lax.rsqrt(ms + 1e-06)).astype(BF16)


def low_half(rows):
    return lax.broadcasted_iota(jnp.int32, (rows, LANES), 1) < HD


def stack_pair(q):
    low = low_half(q.shape[0])
    zero = jnp.zeros_like(q)
    return jnp.concatenate([jnp.where(low, q, zero), jnp.where(low, zero, q)], 0)


def pair_attend(q, k, vext, scales, tile_bias, shifted):
    rows = q.shape[0]
    scores = dot_t(stack_pair(q), k)
    parts, shifts = [], []
    for head in range(2):
        mine = scores[head * rows : (head + 1) * rows]
        biases = tile_bias[head]
        width = k.shape[0] // len(biases)
        tiles = [
            mine[:, t * width : (t + 1) * width] * scales[head] + biases[t]
            for t in range(len(biases))
        ]
        if shifted:
            peak = tiles[0]
            for tile in tiles[1:]:
                peak = jnp.maximum(peak, tile)
            peak = jnp.max(peak, axis=1, keepdims=True)
            shifts.append(peak)
            tiles = [tile - peak for tile in tiles]
        tiles = [jnp.exp2(tile).astype(BF16) for tile in tiles]
        parts.append(tiles[0] if len(tiles) == 1 else jnp.concatenate(tiles, 1))
    got = dot(jnp.concatenate(parts, 0), vext)
    low = low_half(rows)
    total = jnp.where(low, got[:rows, :LANES], got[rows:, :LANES])
    weight = jnp.where(low, got[:rows, LANES:], got[rows:, LANES:])
    return total, weight, shifts


def band_bias(width, distance):
    return 0.0 if distance == 0 else jnp.where(width >= distance, 0.0, OFF).astype(F32)


def plain(factors, first, count):
    flag = factors[first] <= PLAIN_FACTOR
    for i in range(1, count):
        flag = flag & (factors[first + i] <= PLAIN_FACTOR)
    return flag


def token_bias(align, counts, block, first_token_block, window):
    place = lax.broadcasted_iota(jnp.int32, (1, window), 1) // TOKB + first_token_block
    allowed = place == align[block, 0]
    for slot in range(1, ALIST):
        live = jnp.where(slot < counts[block], align[block, slot], -RCH - 1)
        allowed = allowed | (place == live)
    return jnp.where(allowed, 0.0, OFF).astype(F32)


def local_block(f, odd, blocks):
    return jnp.where(odd, f, blocks - 1 - f)


def hidden_kernel(level, frames, table, context, hidden, near, far):
    odd = lax.rem(lax.axis_index("seq"), 2) == 1
    rows, width = frames.shape
    blocks = rows // BLK
    for b in range(blocks):
        at = pl.ds(b * BLK, BLK)
        x = frames[at, :].astype(F32)
        x = x * lax.rsqrt(jnp.mean(x * x, axis=1, keepdims=True) + 1e-06)
        row = table[pl.ds(level[b], 1), :]
        hidden[at, :] = (x * (1.0 + row[:, :width]) + row[:, width:]).astype(BF16)
    halo = WMAX * BLK
    tokens = context.shape[0]
    cwidth = context.shape[1]
    for pack, high in ((near, jnp.logical_not(odd)), (far, odd)):
        start = pl.multiple_of(jnp.where(high, rows - halo, 0), BLK)
        pack[:halo, :] = hidden[pl.ds(start, halo), :]
        start = pl.multiple_of(jnp.where(high, tokens - RCH * TOKB, 0), 16)
        tok = context[pl.ds(start, RCH * TOKB), :]
        pack[halo:, :cwidth] = tok[:TOK_PACK]
        pack[halo : halo + 16, cwidth:] = tok[TOK_PACK:]
        pack[halo + 16 :, cwidth:] = jnp.zeros((TOK_PACK - 16, cwidth), BF16)


def unpack_tokens(pack, halo, cwidth):
    return jnp.concatenate(
        [pack[halo : halo + TOK_PACK, :cwidth], pack[halo : halo + 16, cwidth:]], 0
    )


def main_kernel(
    band,
    factor,
    temp,
    align,
    counts,
    hidden,
    near,
    context,
    wq,
    wk,
    wv,
    wcq,
    wck,
    wcv,
    wo,
    wco,
    out,
    acc_out,
    sum_out,
    peak_out,
    q_out,
    cq_out,
    tok_out,
    window,
    pack,
    tokens,
    keys,
    vext,
    total,
    ready,
    sems,
):
    g = pl.program_id(0)
    device = lax.axis_index("seq")
    odd = lax.rem(device, 2) == 1
    rows = hidden.shape[0]
    blocks = rows // BLK
    halo = WMAX * BLK
    done = blocks - WMAX
    cwidth = context.shape[1]
    own = pl.multiple_of(jnp.where(odd, halo, 0), BLK)
    other = pl.multiple_of(jnp.where(odd, 0, rows), BLK)

    @pl.when(g == 0)
    def _():
        a = pltpu.make_async_copy(hidden, window.at[pl.ds(own, rows)], sems.at[0])
        b = pltpu.make_async_copy(
            near.at[pl.ds(0, halo)], window.at[pl.ds(other, halo)], sems.at[1]
        )
        c = pltpu.make_async_copy(near.at[pl.ds(halo, TOK_PACK)], pack, sems.at[2])
        a.start()
        b.start()
        c.start()
        vext[:, :, LANES:] = jnp.ones((2, window.shape[0], LANES), BF16)
        total[...] = jnp.zeros_like(total)
        tokens[...] = jnp.zeros_like(tokens)
        tokens[RCH * TOKB : RCH * TOKB + context.shape[0], :] = context[...]
        c.wait()
        start = jnp.where(odd, 0, RCH * TOKB + context.shape[0])
        tokens[pl.ds(pl.multiple_of(start, 16), RCH * TOKB), :] = unpack_tokens(pack, 0, cwidth)
        a.wait()
        b.wait()

    mean = head_mean(GCOLS)
    q = head_norm(dot(window[pl.ds(own, rows), :], wq[...]), mean)
    ready[0] = q
    keys[...] = head_norm(dot(window[...], wk[...]), mean)
    values = dot(window[...], wv[...]).astype(BF16)
    for pair in range(2):
        vext[pair, :, :LANES] = values[:, pair * LANES : (pair + 1) * LANES]
    cq = head_norm(dot(window[pl.ds(own, rows), :], wcq[...]), mean[:LANES, :LANES])
    ready[1, :, :LANES] = cq
    ck = head_norm(dot(tokens[...], wck[...]), mean[:LANES, :LANES])
    cv = dot(tokens[...], wcv[...]).astype(BF16)
    cvext = jnp.concatenate([cv, jnp.ones_like(cv)], 1)
    tok_out[...] = tokens[...]
    for f in range(done, blocks):
        start = pl.multiple_of(local_block(f, odd, blocks) * BLK, BLK)
        at = pl.ds((f - done) * BLK, BLK)
        q_out[at, :] = ready[0, pl.ds(start, BLK), :]
        cq_out[at, :] = ready[1, pl.ds(start, BLK), :LANES]

    def self_part(shifted):
        if shifted:

            @pl.when(g == 0)
            def _():
                peak_out[...] = jnp.zeros_like(peak_out)

        outs = [[], []]
        for pair in range(2):
            heads = [g * GROUP + 2 * pair + i for i in range(2)]
            scales = [factor[h] * (HD**-0.5 * LOG2E) for h in heads]
            lanes = slice(pair * LANES, (pair + 1) * LANES)
            for f in range(blocks):
                inner = min(WMAX, blocks - 1 - f)
                count = WMAX + 1 + inner
                start = pl.multiple_of(local_block(f, odd, blocks) * BLK, BLK)
                first = pl.multiple_of(jnp.where(odd, f, blocks - 1 - f - inner) * BLK, BLK)
                at = pl.ds(first, count * BLK)
                bias = [
                    [
                        jnp.where(
                            odd,
                            band_bias(band[h], abs(t - WMAX)),
                            band_bias(band[h], abs(t - inner)),
                        )
                        for t in range(count)
                    ]
                    for h in heads
                ]
                part, weight, shifts = pair_attend(
                    ready[0, pl.ds(start, BLK), lanes],
                    keys[at, lanes],
                    vext[pair, at, :],
                    scales,
                    bias,
                    shifted,
                )
                if f < done:
                    outs[f].append((part / weight).astype(BF16))
                else:
                    to = slice((f - done) * BLK, (f - done + 1) * BLK)
                    acc_out[to, lanes] = part
                    sum_out[to, lanes] = weight
                    if shifted:
                        lane = lax.broadcasted_iota(jnp.int32, (BLK, LANES), 1)
                        peaks = peak_out[to, :]
                        for h, shift in zip(heads, shifts):
                            peaks = jnp.where(lane == h, shift, peaks)
                        peak_out[to, :] = peaks
        mine = jnp.concatenate([jnp.concatenate(o, 1) for o in outs], 0)
        total[...] += dot(mine, wo[...])

    def cross_part(shifted):
        heads = [2 * g, 2 * g + 1]
        scales = [temp[h] * (HD**-0.5 * LOG2E) for h in heads]
        first = device * (context.shape[0] // TOKB) - RCH
        outs = []
        for f in range(done):
            block = local_block(f, odd, blocks)
            start = pl.multiple_of(block * BLK, BLK)
            bias = token_bias(align, counts, block, first, tokens.shape[0])
            part, weight, _ = pair_attend(
                ready[1, pl.ds(start, BLK), :LANES],
                ck,
                cvext,
                scales,
                [[bias], [bias]],
                shifted,
            )
            outs.append((part / weight).astype(BF16))
        total[...] += dot(jnp.concatenate(outs, 0), wco[...])

    easy = plain(factor, g * GROUP, GROUP)
    pl.when(easy)(lambda: self_part(False))
    pl.when(jnp.logical_not(easy))(lambda: self_part(True))
    easy = plain(temp, 2 * g, 2)
    pl.when(easy)(lambda: cross_part(False))
    pl.when(jnp.logical_not(easy))(lambda: cross_part(True))

    @pl.when(g == pl.num_programs(0) - 1)
    def _():
        finish(total, out, window, sems, 0, done, odd, blocks)


def finish(total, out, stage, sems, first, count, odd, blocks):
    copies = []
    for i in range(count):
        at = pl.ds(i * BLK, BLK)
        stage[at, :] = total[at, :].astype(BF16)
        to = pl.multiple_of(local_block(first + i, odd, blocks) * BLK, BLK)
        copies.append(
            pltpu.make_async_copy(stage.at[at], out.at[pl.ds(to, BLK)], sems.at[i])
        )
        copies[-1].start()
    for copy in copies:
        copy.wait()


def tail_kernel(
    blocks,
    band,
    factor,
    temp,
    align,
    counts,
    pack,
    wk,
    wv,
    wck,
    wcv,
    wo,
    wco,
    acc_in,
    sum_in,
    peak_in,
    q_in,
    cq_in,
    tok_in,
    partial_out,
    out,
    tokens,
    keys,
    vext,
    total,
    stage,
    sems,
):
    g = pl.program_id(0)
    device = lax.axis_index("seq")
    odd = lax.rem(device, 2) == 1
    last = lax.axis_size("seq") - 1
    exists = jnp.where(odd, device < last, device > 0)
    halo = WMAX * BLK
    done = blocks - WMAX
    cwidth = tok_in.shape[1]
    window = tok_in.shape[0]

    @pl.when(g == 0)
    def _():
        vext[:, :, LANES:] = jnp.ones((2, halo, LANES), BF16)
        total[...] = jnp.zeros_like(total)
        tokens[...] = tok_in[...]
        start = jnp.where(odd, window - RCH * TOKB, 0)
        tokens[pl.ds(pl.multiple_of(start, 16), RCH * TOKB), :] = unpack_tokens(
            pack, halo, cwidth
        )

    mean = head_mean(GCOLS)
    rows = pack[:halo, :]
    keys[...] = head_norm(dot(rows, wk[...]), mean)
    values = dot(rows, wv[...]).astype(BF16)
    for pair in range(2):
        vext[pair, :, :LANES] = values[:, pair * LANES : (pair + 1) * LANES]
    ck = head_norm(dot(tokens[...], wck[...]), mean[:LANES, :LANES])
    cv = dot(tokens[...], wcv[...]).astype(BF16)
    cvext = jnp.concatenate([cv, jnp.ones_like(cv)], 1)

    def self_part(shifted):
        outs = [[] for _ in range(WMAX)]
        low = low_half(BLK)
        for pair in range(2):
            heads = [g * GROUP + 2 * pair + i for i in range(2)]
            scales = [factor[h] * (HD**-0.5 * LOG2E) for h in heads]
            widths = [jnp.where(exists, band[h], 0) for h in heads]
            lanes = slice(pair * LANES, (pair + 1) * LANES)
            for f in range(done, blocks):
                inner = blocks - 1 - f
                count = WMAX - inner
                first = pl.multiple_of(jnp.where(odd, 0, halo - count * BLK), BLK)
                at = pl.ds(first, count * BLK)
                bias = [
                    [
                        jnp.where(
                            odd,
                            band_bias(w, inner + 1 + t),
                            band_bias(w, inner + count - t),
                        )
                        for t in range(count)
                    ]
                    for w in widths
                ]
                to = slice((f - done) * BLK, (f - done + 1) * BLK)
                part, weight, shifts = pair_attend(
                    q_in[to, lanes], keys[at, lanes], vext[pair, at, :], scales, bias, shifted
                )
                had, had_weight = acc_in[to, lanes], sum_in[to, lanes]
                if shifted:
                    lane = lax.broadcasted_iota(jnp.int32, (BLK, LANES), 1)
                    olds = [
                        jnp.sum(
                            jnp.where(lane == h, peak_in[to, :], 0.0), axis=1, keepdims=True
                        )
                        for h in heads
                    ]
                    news = [jnp.maximum(a, b) for a, b in zip(olds, shifts)]
                    keep = [jnp.exp2(a - n) for a, n in zip(olds, news)]
                    add = [jnp.exp2(b - n) for b, n in zip(shifts, news)]
                    keep = jnp.where(low, keep[0], keep[1])
                    add = jnp.where(low, add[0], add[1])
                    had, had_weight = had * keep, had_weight * keep
                    part, weight = part * add, weight * add
                outs[f - done].append(((had + part) / (had_weight + weight)).astype(BF16))
        mine = jnp.concatenate([jnp.concatenate(o, 1) for o in outs], 0)
        total[...] += dot(mine, wo[...])

    def cross_part(shifted):
        heads = [2 * g, 2 * g + 1]
        scales = [temp[h] * (HD**-0.5 * LOG2E) for h in heads]
        first = device * (window // TOKB - 2 * RCH) - RCH
        outs = []
        for f in range(done, blocks):
            block = local_block(f, odd, blocks)
            bias = token_bias(align, counts, block, first, window)
            to = slice((f - done) * BLK, (f - done + 1) * BLK)
            part, weight, _ = pair_attend(
                cq_in[to, :], ck, cvext, scales, [[bias], [bias]], shifted
            )
            outs.append((part / weight).astype(BF16))
        total[...] += dot(jnp.concatenate(outs, 0), wco[...])

    easy = plain(factor, g * GROUP, GROUP)
    pl.when(easy)(lambda: self_part(False))
    pl.when(jnp.logical_not(easy))(lambda: self_part(True))
    easy = plain(temp, 2 * g, 2)
    pl.when(easy)(lambda: cross_part(False))
    pl.when(jnp.logical_not(easy))(lambda: cross_part(True))

    @pl.when(g == pl.num_programs(0) - 1)
    def _():
        finish(total, out, stage, sems, done, WMAX, odd, blocks)


def shards(
    frames,
    context,
    noise_level,
    alignment,
    counts,
    band_width,
    mod_table,
    qkv_weight,
    out_weight,
    cross_query_weight,
    cross_kv_weight,
    cross_out_weight,
    banded_attender_factor,
    cross_temp,
):
    rows, width = frames.shape
    blocks = rows // BLK
    halo = WMAX * BLK
    done = blocks - WMAX
    tokens, cwidth = context.shape
    query_width = qkv_weight.shape[1] // 3
    cross_width = cross_query_weight.shape[1]
    steps = query_width // GCOLS
    ccols = cross_width // steps
    token_window = tokens + 2 * RCH * TOKB
    devices = lax.axis_size("seq")
    smem = pl.BlockSpec(memory_space=pltpu.SMEM)
    vmem = pl.BlockSpec(memory_space=pltpu.VMEM)
    anywhere = pl.BlockSpec(memory_space=pl.ANY)
    pack_rows = halo + TOK_PACK

    hidden, near, far = pl.pallas_call(
        hidden_kernel,
        out_shape=[
            jax.ShapeDtypeStruct((rows, width), BF16),
            jax.ShapeDtypeStruct((pack_rows, width), BF16),
            jax.ShapeDtypeStruct((pack_rows, width), BF16),
        ],
        in_specs=[smem, vmem, vmem, vmem],
        out_specs=[vmem, vmem, vmem],
        name="hidden_and_packs",
    )(noise_level, frames, mod_table, context)

    same_chip = [(i, i ^ 1) for i in range(devices) if i ^ 1 < devices]
    across = [(i, i + 1) for i in range(1, devices - 1, 2)]
    across += [(b, a) for a, b in across]
    far_got = lax.ppermute(far, "seq", across)
    near_got = lax.ppermute(near, "seq", same_chip)

    def column(block_rows, cols, offset):
        return pl.BlockSpec((block_rows, cols), lambda g: (0, g + offset))

    def row(block_rows, cols):
        return pl.BlockSpec((block_rows, cols), lambda g: (g, 0))

    def whole(*shape):
        return pl.BlockSpec(shape, lambda g: (0,) * len(shape))

    open_rows = WMAX * BLK
    update, acc, weight, peaks, q_open, cq_open, window_tokens = pl.pallas_call(
        main_kernel,
        grid=(steps,),
        out_shape=[
            jax.ShapeDtypeStruct((rows, width), BF16),
            jax.ShapeDtypeStruct((open_rows, query_width), F32),
            jax.ShapeDtypeStruct((open_rows, query_width), F32),
            jax.ShapeDtypeStruct((open_rows, LANES), F32),
            jax.ShapeDtypeStruct((open_rows, query_width), BF16),
            jax.ShapeDtypeStruct((open_rows, cross_width), BF16),
            jax.ShapeDtypeStruct((token_window, cwidth), BF16),
        ],
        in_specs=[smem] * 5
        + [
            anywhere,
            anywhere,
            whole(tokens, cwidth),
            column(width, GCOLS, 0),
            column(width, GCOLS, steps),
            column(width, GCOLS, 2 * steps),
            column(width, ccols, 0),
            column(cwidth, ccols, 0),
            column(cwidth, ccols, steps),
            row(GCOLS, width),
            row(ccols, width),
        ],
        out_specs=[
            anywhere,
            column(open_rows, GCOLS, 0),
            column(open_rows, GCOLS, 0),
            whole(open_rows, LANES),
            column(open_rows, GCOLS, 0),
            column(open_rows, ccols, 0),
            whole(token_window, cwidth),
        ],
        scratch_shapes=[
            pltpu.VMEM((rows + halo, width), BF16),
            pltpu.VMEM((TOK_PACK, width), BF16),
            pltpu.VMEM((token_window, cwidth), BF16),
            pltpu.VMEM((rows + halo, GCOLS), BF16),
            pltpu.VMEM((2, rows + halo, 2 * LANES), BF16),
            pltpu.VMEM((done * BLK, width), F32),
            pltpu.VMEM((2, rows, GCOLS), BF16),
            pltpu.SemaphoreType.DMA((max(3, done),)),
        ],
        compiler_params=pltpu.CompilerParams(vmem_limit_bytes=48 * 2**20),
        cost_estimate=pl.CostEstimate(
            flops=12 * 10**9, bytes_accessed=20 * 10**6, transcendentals=5 * 10**6
        ),
        name="local_attention",
    )(
        band_width,
        banded_attender_factor,
        cross_temp,
        alignment,
        counts,
        hidden,
        near_got,
        context,
        qkv_weight,
        qkv_weight,
        qkv_weight,
        cross_query_weight,
        cross_kv_weight,
        cross_kv_weight,
        out_weight,
        cross_out_weight,
    )

    return pl.pallas_call(
        functools.partial(tail_kernel, blocks),
        grid=(steps,),
        out_shape=jax.ShapeDtypeStruct((rows, width), BF16),
        in_specs=[smem] * 5
        + [
            whole(pack_rows, width),
            column(width, GCOLS, steps),
            column(width, GCOLS, 2 * steps),
            column(cwidth, ccols, 0),
            column(cwidth, ccols, steps),
            row(GCOLS, width),
            row(ccols, width),
            column(open_rows, GCOLS, 0),
            column(open_rows, GCOLS, 0),
            whole(open_rows, LANES),
            column(open_rows, GCOLS, 0),
            column(open_rows, ccols, 0),
            whole(token_window, cwidth),
            anywhere,
        ],
        out_specs=anywhere,
        scratch_shapes=[
            pltpu.VMEM((token_window, cwidth), BF16),
            pltpu.VMEM((halo, GCOLS), BF16),
            pltpu.VMEM((2, halo, 2 * LANES), BF16),
            pltpu.VMEM((open_rows, width), F32),
            pltpu.VMEM((open_rows, width), BF16),
            pltpu.SemaphoreType.DMA((WMAX,)),
        ],
        input_output_aliases={18: 0},
        compiler_params=pltpu.CompilerParams(vmem_limit_bytes=48 * 2**20),
        cost_estimate=pl.CostEstimate(
            flops=5 * 10**9, bytes_accessed=12 * 10**6, transcendentals=10**6
        ),
        name="halo_attention",
    )(
        band_width,
        banded_attender_factor,
        cross_temp,
        alignment,
        counts,
        far_got,
        qkv_weight,
        qkv_weight,
        cross_kv_weight,
        cross_kv_weight,
        out_weight,
        cross_out_weight,
        acc,
        weight,
        peaks,
        q_open,
        cq_open,
        window_tokens,
        update,
    )


def solution(mesh):
    placed = (
        P(("groups", "seq"), None),
        P(("groups", "seq"), None),
        P(("groups", "seq")),
        P(("groups", "seq"), None),
        P(("groups", "seq")),
        P(),
        P(),
        P(),
        P(),
        P(),
        P(),
        P(),
        P(),
        P(),
    )
    return jax.shard_map(
        shards, mesh=mesh, in_specs=placed, out_specs=P(("groups", "seq"), None), check_vma=False
    )
```

time: 134 us -> 59 us (0.44)
  matrix products: 53.7 us -> 0 us
  Pallas kernels: 0 us -> 47.4 us
  local copies, waits for them, and re-layouts: 40.2 us -> 6.74 us
  other arithmetic: 25.8 us -> 0 us
  starting transfers between devices: 12.3 us -> 4.53 us
    pallas_call x0 -> x3, Pallas kernels: none -> 47.4 us  [the longest x1 29.9 us: shards(): pl.pallas_call(main_kernel, grid=(steps,), out_shape=[jax.ShapeDtypeStruc...]
    dot_general x9 -> x0, matrix products: 31.9 us -> none  [the longest x1 13.9 us: attend(): jnp.einsum('hij,jhd->ihd', weights, value_rows, preferred_element_type=jn...]
    sub x1 -> x0, matrix products: 21.8 us -> none  [masked_softmax(): powers = jnp.exp(scores - peak)]
    mul x9 -> x0, local copies, waits for them, and re-layouts: 17.8 us -> none  [the longest x6 11 us: head_norm(): parts * lax.rsqrt(jnp.mean(parts * parts, axis=-1, keepdims=True) + 1e-06)]
    slice x7 -> x0, local copies, waits for them, and re-layouts: 15.3 us -> none  [the longest x2 6.37 us: attend(): key_rows = key_pairs[:, :query_width].reshape(-1, BANDED_ATTEND_CT, HD)]
    ppermute x4 -> x2, starting transfers between devices: 12.3 us -> 4.53 us  [the longest x1 4.47 us: shards(): far_got = lax.ppermute(far, 'seq', across)]
    convert_element_type x3 -> x0, other arithmetic: 7.36 us -> none  [the longest x1 5.25 us: shards(): head_norm(projected[:, :query_width], BANDED_ATTEND_CT).astype(jnp.bfloat16)]
    reduce_sum x4 -> x0, other arithmetic: 6.35 us -> none  [the longest x3 4.85 us: head_norm(): jnp.mean(parts * parts, axis=-1, keepdims=True) + 1e-06]
  transfers between devices with their start and end apart: 4 -> 2, of which waited for: 0 -> 0; matrix products, arithmetic and copies ran while one was open for 50% -> 1% of each run, Pallas kernels for 0% -> 51%
where the time goes in v1:
time: 59 us; the launch traced here: 58.7 us
  Pallas kernels  47.4 us (80%)
  local copies, waits for them, and re-layouts  6.74 us (11%)
  starting transfers between devices  4.53 us (8%)
    pallas_call x1, Pallas kernels, shards(): pl.pallas_call(main_kernel, grid=(steps,), out_shape=[jax.ShapeDtypeStruc...  29.9 us
    pallas_call x1, Pallas kernels, shards(): pl.pallas_call(functools.partial(tail_kernel, blocks), grid=(steps,), out...  14.2 us
    unnamed x19, local copies, waits for them, and re-layouts  6.74 us
    ppermute x1, starting transfers between devices, shards(): far_got = lax.ppermute(far, 'seq', across)  4.47 us
    pallas_call x1, Pallas kernels, shards(): pl.pallas_call(hidden_kernel, out_shape=[jax.ShapeDtypeStruct((rows, widt...  3.24 us
  transfers between devices with their start and end apart: 2, of which 0 were waited for; matrix products, arithmetic and copies ran while one was open for 1% of the time, Pallas kernels for 51%

profile of v1, /device:TPU:1, one launch (start us, length us, event | category | flops | bytes accessed | tf_op | source)
XLA Modules:
  0.0 58.7 jit_solution(17832112160645000104)
XLA Ops:
  0.0 3.2 %hidden_and_packs.1 = (bf16[512,1024]{1,0:T(8,128)(2,1)}, bf16[288,1024]{1,0:T(8,128)(2,1)}, bf16[288,1024]{1,0:T(8,128)(2,1)}) custom-call(s32[4]{0:T(128)} %level.1, bf16[512,1024]{1,0:T(8,128)(2,1)} %frames.1, f32[8,2048]{1,0:T(8,128)} %table.1, bf16[96,512]{1,0:T(8,128)(2,1)} %context.3), custom_call_target="tpu_custom_call" | custom-call | tf_op jit(solution)/shard_map/hidden_and_packs/pallas_call | solution.py:491
  3.2 0.1 collective-permute-start.1
  3.3 4.5 %collective-permute-start = (bf16[288,1024]{1,0:T(8,128)(2,1)}, bf16[288,1024]{1,0:T(8,128)(2,1)S(1)}, u32[]{:S(2)}, u32[]{:S(2)}) collective-permute-start(bf16[288,1024]{1,0:T(8,128)(2,1)} %get-tuple-element.15), channel_id=1, source_target_pairs={{1,2},{3,4},{5,6},{7,8},{9,10},{11,12},{13,14},{2,1},{4,3},{6,5},{... | collective-permute-start | bytes 1769480 | tf_op jit(solution)/shard_map/ppermute | solution.py:506
  7.8 0.8 %copy.17.align = s32[4,2]{1,0:T(4,128)S(1)} copy(s32[4,2]{0,1:T(2,128)} %param.17) | data formatting | bytes 64 | tf_op args[3]
  8.6 0.0 collective-permute-done.1.near
  8.6 0.0 copy-start.2
  8.6 0.9 %copy-done.2 = bf16[96,512]{1,0:T(8,128)(2,1)S(1)} copy-done((bf16[96,512]{1,0:T(8,128)(2,1)S(1)}, bf16[96,512]{1,0:T(8,128)(2,1)}, u32[]{:S(2)}) %copy-start.2) | copy-done | bytes 98328
  9.4 0.0 copy-start.3
  9.4 0.7 %copy-done.3 = s32[16]{0:T(128)S(1)} copy-done((s32[16]{0:T(128)S(1)}, s32[16]{0:T(128)}, u32[]{:S(2)}) %copy-start.3) | copy-done | bytes 88
  10.1 0.0 copy-start.4
  10.1 0.7 %copy-done.4 = f32[16]{0:T(128)S(1)} copy-done((f32[16]{0:T(128)S(1)}, f32[16]{0:T(128)}, u32[]{:S(2)}) %copy-start.4) | copy-done | bytes 88
  10.8 0.0 copy-start.5
  10.8 0.7 %copy-done.5 = f32[8]{0:T(128)S(1)} copy-done((f32[8]{0:T(128)S(1)}, f32[8]{0:T(128)}, u32[]{:S(2)}) %copy-start.5) | copy-done | bytes 56
  11.4 0.0 copy-start.6
  11.4 0.7 %copy-done.6 = s32[4]{0:T(128)S(1)} copy-done((s32[4]{0:T(128)S(1)}, s32[4]{0:T(128)}, u32[]{:S(2)}) %copy-start.6) | copy-done | bytes 40
  12.1 0.0 copy-start.7
  12.1 1.2 %copy-done.7 = bf16[1024,512]{1,0:T(8,128)(2,1)S(1)} copy-done((bf16[1024,512]{1,0:T(8,128)(2,1)S(1)}, bf16[1024,512]{1,0:T(8,128)(2,1)}, u32[]{:S(2)}) %copy-start.7) | copy-done | bytes 1048600
  13.3 0.0 copy-start.8
  13.3 1.2 %copy-done.8 = bf16[512,1024]{1,0:T(8,128)(2,1)S(1)} copy-done((bf16[512,1024]{1,0:T(8,128)(2,1)S(1)}, bf16[512,1024]{1,0:T(8,128)(2,1)}, u32[]{:S(2)}) %copy-start.8) | copy-done | bytes 1048600
  14.5 0.0 copy-start
  14.5 0.0 copy-start.1
  14.5 29.9 %local_attention.1 = (bf16[512,1024]{1,0:T(8,128)(2,1)}, f32[256,1024]{1,0:T(8,128)S(1)}, f32[256,1024]{1,0:T(8,128)S(1)}, f32[256,128]{1,0:T(8,128)S(1)}, bf16[...) custom-call(s32[16]{0:T(128)S(1)} %copy-done.3, f32[16]{0:T(128)S(1)} %copy-done.4, ...), custom_call_target="tpu_custom_call" | custom-call | flops 12000000000 | bytes 20000000 | tf_op jit(solution)/shard_map/local_attention/pallas_call | solution.py:519
  44.5 0.0 collective-permute-done.pack
  44.5 0.0 copy-done
  44.5 0.0 copy-done.1
  44.5 14.2 %halo_attention.1 = bf16[512,1024]{1,0:T(8,128)(2,1)} custom-call(s32[16]{0:T(128)S(1)} %copy-done.3, f32[16]{0:T(128)S(1)} %copy-done.4, f32[8]{0:T(128)S(1)} %copy-done.5, s32[4,2]{1,0:T(4,128)S(1)} %copy.17.align, s32[4]{0:T(128)S(1)} %copy-done.6, bf16[288,1024]{1,0:T(8,128)(2,1)S(1)} %collective-permute-done.pack, ...), custom_call_target="tpu_custom_call", output_to_operand_aliasing={{}: (18, {})} | custom-call | flops 5000000000 | bytes 12000000 | tf_op jit(solution)/shard_map/halo_attention/pallas_call | solution.py:588
Async XLA Ops:
  3.2 5.3 %collective-permute-start.1 = (bf16[288,1024]{1,0:T(8,128)(2,1)}, bf16[288,1024]{1,0:T(8,128)(2,1)S(1)}, u32[]{:S(2)}, u32[]{:S(2)}) collective-permute-start(bf16[288,1024]{1,0:T(8,128)(2,1)} %get-tuple-element.17), channel_id=1, source_target_pairs={{0,1},{1,0},{2,3},{3,2},{4,5},{5,4},{6,7},{7,6},{8,9},{9,8},{10,11... | collective-permute-start | bytes 1769480 | tf_op jit(solution)/shard_map/ppermute | solution.py:507
  3.3 41.2 %collective-permute-start = (bf16[288,1024]{1,0:T(8,128)(2,1)}, bf16[288,1024]{1,0:T(8,128)(2,1)S(1)}, u32[]{:S(2)}, u32[]{:S(2)}) collective-permute-start(bf16[288,1024]{1,0:T(8,128)(2,1)} %get-tuple-element.15), channel_id=1, source_target_pairs={{1,2},{3,4},{5,6},{7,8},{9,10},{11,12},{13,14},{2,1},{4,3},{6,5},{... | collective-permute-start | bytes 1769480 | tf_op jit(solution)/shard_map/ppermute | solution.py:506
  8.6 0.9 %copy-start.2 = (bf16[96,512]{1,0:T(8,128)(2,1)S(1)}, bf16[96,512]{1,0:T(8,128)(2,1)}, u32[]{:S(2)}) copy-start(bf16[96,512]{1,0:T(8,128)(2,1)} %context.3) | copy-start | bytes 294916
  9.4 0.7 %copy-start.3 = (s32[16]{0:T(128)S(1)}, s32[16]{0:T(128)}, u32[]{:S(2)}) copy-start(s32[16]{0:T(128)} %band.3) | copy-start | bytes 196
  10.1 0.7 %copy-start.4 = (f32[16]{0:T(128)S(1)}, f32[16]{0:T(128)}, u32[]{:S(2)}) copy-start(f32[16]{0:T(128)} %factor.3) | copy-start | bytes 196
  10.8 0.7 %copy-start.5 = (f32[8]{0:T(128)S(1)}, f32[8]{0:T(128)}, u32[]{:S(2)}) copy-start(f32[8]{0:T(128)} %temp.3) | copy-start | bytes 100
  11.4 0.7 %copy-start.6 = (s32[4]{0:T(128)S(1)}, s32[4]{0:T(128)}, u32[]{:S(2)}) copy-start(s32[4]{0:T(128)} %counts.3) | copy-start | bytes 52
  12.1 1.2 %copy-start.7 = (bf16[1024,512]{1,0:T(8,128)(2,1)S(1)}, bf16[1024,512]{1,0:T(8,128)(2,1)}, u32[]{:S(2)}) copy-start(bf16[1024,512]{1,0:T(8,128)(2,1)} %wcq.1) | copy-start | bytes 3145732
  13.3 1.2 %copy-start.8 = (bf16[512,1024]{1,0:T(8,128)(2,1)S(1)}, bf16[512,1024]{1,0:T(8,128)(2,1)}, u32[]{:S(2)}) copy-start(bf16[512,1024]{1,0:T(8,128)(2,1)} %get-tuple-element.16.hidden) | copy-start | bytes 3145732
  14.5 30.0 %copy-start = (bf16[512,1024]{1,0:T(8,128)(2,1)S(1)}, bf16[512,1024]{1,0:T(8,128)(2,1)}, u32[]{:S(2)}) copy-start(bf16[512,1024]{1,0:T(8,128)(2,1)} %wcv.3) | copy-start | bytes 3145732
  14.5 30.0 %copy-start.1 = (bf16[512,1024]{1,0:T(8,128)(2,1)S(1)}, bf16[512,1024]{1,0:T(8,128)(2,1)}, u32[]{:S(2)}) copy-start(bf16[512,1024]{1,0:T(8,128)(2,1)} %wco.3) | copy-start | bytes 3145732

commit v2 on v0

v2 whole, which is shorter than its diff:
```python
import jax
import jax.numpy as jnp
from jax import lax
from jax.experimental import pallas as pl
from jax.experimental.pallas import tpu as pltpu
from jax.sharding import PartitionSpec as P

BANDED_ATTEND_CT = 16
MIXED_ATTEND_CNT = 8
HD = 64
LEVELS = 8
BLK = 128
WMAX = 2
TOKB = 48
RCH = 1
ALIST = 2

LANES = 128
CHUNK = 512
TILE = 256
LOG2E = 1.4426950408889634
OFF = -1e30
PLAIN_FACTOR = 8.0
F32 = jnp.float32
BF16 = jnp.bfloat16
MAIN_VMEM = 32 * 2**20
TAIL_VMEM = 16 * 2**20
TOK_PACK = 32


def dot(a, b):
    return jnp.dot(a, b, preferred_element_type=F32)


def dot_t(a, b):
    return lax.dot_general(a, b, (((1,), (1,)), ((), ())), preferred_element_type=F32)


def low_half(rows):
    return lax.broadcasted_iota(jnp.int32, (rows, LANES), 1) < HD


def head_norm(x):
    low = low_half(x.shape[0])
    done = []
    for start in range(0, x.shape[1], LANES):
        pair = x[:, start : start + LANES]
        square = pair * pair
        first = jnp.sum(jnp.where(low, square, 0.0), axis=1, keepdims=True)
        second = jnp.sum(jnp.where(low, 0.0, square), axis=1, keepdims=True)
        mean = jnp.where(low, first, second) * (1.0 / HD)
        done.append((pair * lax.rsqrt(mean + 1e-06)).astype(BF16))
    return jnp.concatenate(done, 1)


def staggered(items, delay=1):
    begun = []
    for begin, end in items:
        begun.append((end, begin()))
        if len(begun) > delay:
            end, value = begun.pop(0)
            end(value)
    for end, value in begun:
        end(value)


def pair_scores(q, k):
    low = low_half(q.shape[0])
    zero = jnp.zeros_like(q)
    stacked = jnp.concatenate([jnp.where(low, q, zero), jnp.where(low, zero, q)], 0)
    return dot_t(stacked, k)


def pair_sums(scores, vext, scales, tile_bias, shifted):
    rows = scores.shape[0] // 2
    parts, shifts = [], []
    for head in range(2):
        mine = scores[head * rows : (head + 1) * rows]
        biases = tile_bias[head]
        width = mine.shape[1] // len(biases)
        tiles = []
        for t, bias in enumerate(biases):
            tile = mine[:, t * width : (t + 1) * width] * scales[head]
            tiles.append(tile if bias is None else tile + bias)
        if shifted:
            peak = tiles[0]
            for tile in tiles[1:]:
                peak = jnp.maximum(peak, tile)
            peak = jnp.max(peak, axis=1, keepdims=True)
            shifts.append(peak)
            tiles = [tile - peak for tile in tiles]
        tiles = [jnp.exp2(tile).astype(BF16) for tile in tiles]
        parts.append(tiles[0] if len(tiles) == 1 else jnp.concatenate(tiles, 1))
    got = dot(jnp.concatenate(parts, 0), vext)
    low = low_half(rows)
    total = jnp.where(low, got[:rows, :LANES], got[rows:, :LANES])
    weight = jnp.where(low, got[:rows, LANES:], got[rows:, LANES:])
    return total, weight, shifts


def band_bias(width, distance):
    return jnp.where(width >= distance, 0.0, OFF).astype(F32)


def plain(factor, temp):
    flag = factor[0] <= PLAIN_FACTOR
    for i in range(1, BANDED_ATTEND_CT):
        flag = flag & (factor[i] <= PLAIN_FACTOR)
    for i in range(MIXED_ATTEND_CNT):
        flag = flag & (temp[i] <= PLAIN_FACTOR)
    return flag


def token_bias(align, counts, block, first_token_block, window):
    place = lax.broadcasted_iota(jnp.int32, (1, window), 1) // TOKB + first_token_block
    allowed = place == align[0, block]
    for slot in range(1, ALIST):
        live = jnp.where(slot < counts[block], align[slot, block], -RCH - 1)
        allowed = allowed | (place == live)
    return jnp.where(allowed, 0.0, OFF).astype(F32)


def local_block(f, odd, blocks):
    return jnp.where(odd, f, blocks - 1 - f)


def in_hbm(*arrays):
    return [pltpu.with_memory_space_constraint(a, pltpu.HBM) for a in arrays]


def lanes_of(pair):
    if isinstance(pair, int):
        return slice(pair * LANES, (pair + 1) * LANES)
    return pl.ds(pl.multiple_of(pair * LANES, LANES), LANES)


def hidden_kernel(level, frames, table, context, hidden, near, far, stage, sems):
    odd = lax.rem(lax.axis_index("seq"), 2) == 1
    rows, width = frames.shape
    blocks = rows // BLK
    copies = []
    for b in range(blocks):
        at = pl.ds(b * BLK, BLK)
        copies.append(pltpu.make_async_copy(frames.at[at], stage.at[at], sems.at[b]))
        copies[-1].start()
    for b in range(blocks):
        at = pl.ds(b * BLK, BLK)
        row = table[pl.ds(level[b], 1), :]
        copies[b].wait()
        x = stage[at, :].astype(F32)
        x = x * lax.rsqrt(jnp.mean(x * x, axis=1, keepdims=True) + 1e-06)
        hidden[at, :] = (x * (1.0 + row[:, :width]) + row[:, width:]).astype(BF16)
    halo = WMAX * BLK
    tokens = context.shape[0]
    cwidth = context.shape[1]
    for pack, high in ((near, jnp.logical_not(odd)), (far, odd)):
        start = pl.multiple_of(jnp.where(high, rows - halo, 0), BLK)
        pack[:halo, :] = hidden[pl.ds(start, halo), :]
        start = pl.multiple_of(jnp.where(high, tokens - RCH * TOKB, 0), 16)
        tok = context[pl.ds(start, RCH * TOKB), :]
        pack[halo:, :cwidth] = tok[:TOK_PACK]
        pack[halo : halo + 16, cwidth:] = tok[TOK_PACK:]
        pack[halo + 16 :, cwidth:] = jnp.zeros((TOK_PACK - 16, cwidth), BF16)


def unpack_tokens(pack, halo, cwidth):
    return jnp.concatenate(
        [pack[halo : halo + TOK_PACK, :cwidth], pack[halo : halo + 16, cwidth:]], 0
    )


def token_pairs(tokens, wckv, ck, cvext):
    cwidth = ck.shape[1]
    x = tokens[...]
    ck[...] = head_norm(dot(x, wckv[:, :cwidth]))
    values = dot(x, wckv[:, cwidth:]).astype(BF16)
    for pair in range(cwidth // LANES):
        cvext[pair, :, :LANES] = values[:, lanes_of(pair)]


def store_values(vext, at, start, values):
    for i in range(values.shape[1] // LANES):
        vext[start // LANES + i, at, :LANES] = values[:, lanes_of(i)]


def scalar_copies(sources, targets, sems, first):
    copies = []
    for i, (source, target) in enumerate(zip(sources, targets)):
        copies.append(pltpu.make_async_copy(source, target, sems.at[first + i]))
        copies[-1].start()
    return copies


def finish(total, out, stage, sems, first, count, odd, blocks):
    copies = []
    for i in range(count):
        at = pl.ds(i * BLK, BLK)
        stage[at, :] = total[i * BLK : (i + 1) * BLK].astype(BF16)
        to = pl.multiple_of(local_block(first + i, odd, blocks) * BLK, BLK)
        copies.append(
            pltpu.make_async_copy(stage.at[at], out.at[pl.ds(to, BLK)], sems.at[i])
        )
        copies[-1].start()
    for copy in copies:
        copy.wait()


def main_kernel(
    band_in,
    factor_in,
    temp_in,
    align_in,
    counts_in,
    hidden,
    near,
    context,
    wqkv_in,
    wcq_in,
    wckv_in,
    wo_in,
    wco_in,
    out,
    acc_out,
    sum_out,
    peak_out,
    q,
    cq,
    band,
    factor,
    temp,
    align,
    counts,
    wqkv,
    wcq,
    wckv,
    wo,
    wco,
    tokens,
    keys,
    vext,
    ck,
    cvext,
    mine,
    cross_mine,
    stage,
    sems,
):
    device = lax.axis_index("seq")
    odd = lax.rem(device, 2) == 1
    rows = hidden.shape[0]
    blocks = rows // BLK
    halo = WMAX * BLK
    done = blocks - WMAX
    qwidth = q.shape[1]
    cwidth = context.shape[1]
    own = jnp.where(odd, halo, 0)
    other = jnp.where(odd, 0, rows)

    loads = []
    for start in range(0, 3 * qwidth, CHUNK):
        cols = pl.ds(start, CHUNK)
        loads.append((wqkv_in.at[:, cols], wqkv.at[:, cols]))
    loads += [(wcq_in, wcq), (wckv_in, wckv), (wo_in, wo), (wco_in, wco)]
    loads = [pltpu.make_async_copy(a, b, sems.at[i]) for i, (a, b) in enumerate(loads)]
    for load in loads[:2]:
        load.start()
    scalars = scalar_copies(
        (band_in, factor_in, temp_in, align_in, counts_in),
        (band, factor, temp, align, counts),
        sems,
        len(loads),
    )
    for load in loads[2:]:
        load.start()

    vext[:, :, LANES:] = jnp.ones((vext.shape[0], vext.shape[1], LANES), BF16)
    cvext[:, :, LANES:] = jnp.ones((cvext.shape[0], cvext.shape[1], LANES), BF16)
    tokens[...] = jnp.zeros_like(tokens)
    tokens[RCH * TOKB : RCH * TOKB + context.shape[0], :] = context[...]
    start = jnp.where(odd, 0, RCH * TOKB + context.shape[0])
    tokens[pl.ds(pl.multiple_of(start, 16), RCH * TOKB), :] = unpack_tokens(near, halo, cwidth)

    def project(source, first, to, start):
        def begin():
            return dot(source[first : first + TILE, :], wqkv[:, start : start + CHUNK])

        def end(x):
            at = pl.ds(pl.multiple_of(to + first, BLK), TILE)
            part, col = divmod(start, qwidth)
            if part == 0:
                q[first : first + TILE, col : col + CHUNK] = head_norm(x)
            elif part == 1:
                keys[at, col : col + CHUNK] = head_norm(x)
            else:
                store_values(vext, at, col, x.astype(BF16))

        return begin, end

    def project_cross(first):
        def begin():
            return dot(hidden[first : first + TILE, :], wcq[...])

        def end(x):
            cq[first : first + TILE, :] = head_norm(x)

        return begin, end

    items = []
    for i, start in enumerate(range(0, 3 * qwidth, CHUNK)):
        tiles = [project(hidden, first, own, start) for first in range(0, rows, TILE)]
        if start >= qwidth:
            tiles += [project(near, first, other, start) for first in range(0, halo, TILE)]
        begin, end = tiles[0]
        tiles[0] = (lambda i=i, begin=begin: (loads[i].wait(), begin())[1], end)
        items += tiles
    staggered(items)
    count = 3 * qwidth // CHUNK
    loads[count].wait()
    loads[count + 1].wait()
    staggered([project_cross(first) for first in range(0, rows, TILE)])
    token_pairs(tokens, wckv, ck, cvext)
    for copy in scalars:
        copy.wait()

    def self_item(pair, f, shifted):
        heads = [2 * pair, 2 * pair + 1]
        lanes = lanes_of(pair)
        inner = min(WMAX, blocks - 1 - f)
        count = WMAX + 1 + inner
        start = pl.multiple_of(local_block(f, odd, blocks) * BLK, BLK)
        first = pl.multiple_of(jnp.where(odd, f, blocks - 1 - f - inner) * BLK, BLK)
        at = pl.ds(first, count * BLK)

        def begin():
            return pair_scores(q[pl.ds(start, BLK), lanes], keys[at, lanes])

        def end(scores):
            bias = [[] for _ in heads]
            for mine_bias, h in zip(bias, heads):
                by_distance = [0.0] + [band_bias(band[h], d) for d in range(1, WMAX + 1)]
                for t in range(count):
                    one, two = abs(t - WMAX), abs(t - inner)
                    if one == two:
                        mine_bias.append(None if one == 0 else by_distance[one])
                    else:
                        mine_bias.append(jnp.where(odd, by_distance[one], by_distance[two]))
            scales = [factor[h] * (HD**-0.5 * LOG2E) for h in heads]
            part, weight, shifts = pair_sums(scores, vext[pair, at, :], scales, bias, shifted)
            if f < done:
                mine[f * BLK : (f + 1) * BLK, lanes] = (part / weight).astype(BF16)
                return
            to = slice((f - done) * BLK, (f - done + 1) * BLK)
            acc_out[to, lanes] = part
            sum_out[to, lanes] = weight
            if shifted:
                lane = lax.broadcasted_iota(jnp.int32, (BLK, LANES), 1)
                peaks = peak_out[to, :]
                for h, shift in zip(heads, shifts):
                    peaks = jnp.where(lane == h, shift, peaks)
                peak_out[to, :] = peaks

        return begin, end

    biases = [
        token_bias(
            align,
            counts,
            local_block(f, odd, blocks),
            device * (context.shape[0] // TOKB) - RCH,
            tokens.shape[0],
        )
        for f in range(done)
    ]

    def cross_item(pair, f, shifted):
        lanes = lanes_of(pair)
        start = pl.multiple_of(local_block(f, odd, blocks) * BLK, BLK)

        def begin():
            return pair_scores(cq[pl.ds(start, BLK), lanes], ck[:, lanes])

        def end(scores):
            scales = [temp[2 * pair + i] * (HD**-0.5 * LOG2E) for i in range(2)]
            part, weight, _ = pair_sums(
                scores, cvext[pair], scales, [[biases[f]]] * 2, shifted
            )
            cross_mine[f * BLK : (f + 1) * BLK, lanes] = (part / weight).astype(BF16)

        return begin, end

    pairs, cross_pairs = qwidth // LANES, cwidth // LANES
    easy = plain(factor, temp)

    @pl.when(easy)
    def _():
        items = [cross_item(p, f, False) for p in range(cross_pairs) for f in range(done)]
        items += [self_item(p, f, False) for p in range(pairs) for f in range(blocks)]
        staggered(items)

    @pl.when(jnp.logical_not(easy))
    def _():
        peak_out[...] = jnp.zeros_like(peak_out)

        @pl.loop(0, pairs)
        def _(p):
            staggered([self_item(p, f, True) for f in range(blocks)])

        @pl.loop(0, cross_pairs)
        def _(p):
            staggered([cross_item(p, f, True) for f in range(done)])

    for load in loads[count + 2 :]:
        load.wait()
    total = dot(mine[...], wo[...]) + dot(cross_mine[...], wco[...])
    finish(total, out, stage, sems, 0, done, odd, blocks)


def tail_kernel(
    band_in,
    factor_in,
    temp_in,
    align_in,
    counts_in,
    pack,
    near,
    context,
    wqkv,
    wckv,
    wo,
    wco,
    acc_in,
    sum_in,
    peak_in,
    q,
    cq,
    partial_out,
    out,
    band,
    factor,
    temp,
    align,
    counts,
    tokens,
    keys,
    vext,
    ck,
    cvext,
    mine,
    cross_mine,
    stage,
    sems,
):
    device = lax.axis_index("seq")
    odd = lax.rem(device, 2) == 1
    last = lax.axis_size("seq") - 1
    exists = jnp.where(odd, device < last, device > 0)
    rows, qwidth = q.shape
    blocks = rows // BLK
    halo = WMAX * BLK
    done = blocks - WMAX
    cwidth = context.shape[1]
    window = tokens.shape[0]

    scalars = scalar_copies(
        (band_in, factor_in, temp_in, align_in, counts_in),
        (band, factor, temp, align, counts),
        sems,
        WMAX,
    )
    vext[:, :, LANES:] = jnp.ones((vext.shape[0], vext.shape[1], LANES), BF16)
    cvext[:, :, LANES:] = jnp.ones((cvext.shape[0], cvext.shape[1], LANES), BF16)
    tokens[RCH * TOKB : RCH * TOKB + context.shape[0], :] = context[...]
    ends = [jnp.where(odd, 0, window - RCH * TOKB), jnp.where(odd, window - RCH * TOKB, 0)]
    for start, source in zip(ends, (near, pack)):
        at = pl.ds(pl.multiple_of(start, 16), RCH * TOKB)
        tokens[at, :] = unpack_tokens(source, halo, cwidth)

    def project(first, start):
        def begin():
            return dot(pack[first : first + TILE, :], wqkv[:, start : start + CHUNK])

        def end(x):
            part, col = divmod(start, qwidth)
            at = slice(first, first + TILE)
            if part == 1:
                keys[at, col : col + CHUNK] = head_norm(x)
            else:
                store_values(vext, at, col, x.astype(BF16))

        return begin, end

    staggered(
        [
            project(first, start)
            for start in range(qwidth, 3 * qwidth, CHUNK)
            for first in range(0, halo, TILE)
        ]
    )
    token_pairs(tokens, wckv, ck, cvext)
    for copy in scalars:
        copy.wait()

    def self_item(pair, f, shifted):
        heads = [2 * pair, 2 * pair + 1]
        lanes = lanes_of(pair)
        inner = blocks - 1 - f
        count = WMAX - inner
        start = pl.multiple_of(local_block(f, odd, blocks) * BLK, BLK)
        first = pl.multiple_of(jnp.where(odd, 0, halo - count * BLK), BLK)
        at = pl.ds(first, count * BLK)

        def begin():
            return pair_scores(q[pl.ds(start, BLK), lanes], keys[at, lanes])

        def end(scores):
            bias = [[] for _ in heads]
            for mine_bias, h in zip(bias, heads):
                width = jnp.where(exists, band[h], 0)
                for t in range(count):
                    one, two = band_bias(width, inner + 1 + t), band_bias(width, inner + count - t)
                    mine_bias.append(jnp.where(odd, one, two))
            scales = [factor[h] * (HD**-0.5 * LOG2E) for h in heads]
            part, weight, shifts = pair_sums(scores, vext[pair, at, :], scales, bias, shifted)
            to = slice((f - done) * BLK, (f - done + 1) * BLK)
            had, had_weight = acc_in[to, lanes], sum_in[to, lanes]
            if shifted:
                low = low_half(BLK)
                lane = lax.broadcasted_iota(jnp.int32, (BLK, LANES), 1)
                olds = [
                    jnp.sum(jnp.where(lane == h, peak_in[to, :], 0.0), axis=1, keepdims=True)
                    for h in heads
                ]
                news = [jnp.maximum(a, b) for a, b in zip(olds, shifts)]
                keep = [jnp.exp2(a - n) for a, n in zip(olds, news)]
                add = [jnp.exp2(b - n) for b, n in zip(shifts, news)]
                keep = jnp.where(low, keep[0], keep[1])
                add = jnp.where(low, add[0], add[1])
                had, had_weight = had * keep, had_weight * keep
                part, weight = part * add, weight * add
            mine[to, lanes] = ((had + part) / (had_weight + weight)).astype(BF16)

        return begin, end

    biases = [
        token_bias(
            align,
            counts,
            local_block(f, odd, blocks),
            device * (context.shape[0] // TOKB) - RCH,
            window,
        )
        for f in range(done, blocks)
    ]

    def cross_item(pair, f, shifted):
        lanes = lanes_of(pair)
        start = pl.multiple_of(local_block(f, odd, blocks) * BLK, BLK)

        def begin():
            return pair_scores(cq[pl.ds(start, BLK), lanes], ck[:, lanes])

        def end(scores):
            scales = [temp[2 * pair + i] * (HD**-0.5 * LOG2E) for i in range(2)]
            part, weight, _ = pair_sums(
                scores, cvext[pair], scales, [[biases[f - done]]] * 2, shifted
            )
            to = slice((f - done) * BLK, (f - done + 1) * BLK)
            cross_mine[to, lanes] = (part / weight).astype(BF16)

        return begin, end

    pairs, cross_pairs = qwidth // LANES, cwidth // LANES
    easy = plain(factor, temp)

    @pl.when(easy)
    def _():
        items = [
            cross_item(p, f, False) for p in range(cross_pairs) for f in range(done, blocks)
        ]
        items += [self_item(p, f, False) for p in range(pairs) for f in range(done, blocks)]
        staggered(items, 2)

    @pl.when(jnp.logical_not(easy))
    def _():
        @pl.loop(0, pairs)
        def _(p):
            staggered([self_item(p, f, True) for f in range(done, blocks)])

        @pl.loop(0, cross_pairs)
        def _(p):
            staggered([cross_item(p, f, True) for f in range(done, blocks)])

    total = dot(mine[...], wo[...]) + dot(cross_mine[...], wco[...])
    finish(total, out, stage, sems, done, WMAX, odd, blocks)


def shards(
    frames,
    context,
    noise_level,
    alignment,
    counts,
    band_width,
    mod_table,
    qkv_weight,
    out_weight,
    cross_query_weight,
    cross_kv_weight,
    cross_out_weight,
    banded_attender_factor,
    cross_temp,
):
    rows, width = frames.shape
    blocks = rows // BLK
    halo = WMAX * BLK
    done = blocks - WMAX
    tokens, cwidth = context.shape
    qwidth = qkv_weight.shape[1] // 3
    cqwidth = cross_query_weight.shape[1]
    pairs, cross_pairs = qwidth // LANES, cqwidth // LANES
    window = tokens + 2 * RCH * TOKB
    devices = lax.axis_size("seq")
    smem = pl.BlockSpec(memory_space=pltpu.SMEM)
    vmem = pl.BlockSpec(memory_space=pltpu.VMEM)
    hbm = pl.BlockSpec(memory_space=pltpu.HBM)
    pack_rows = halo + TOK_PACK

    hidden, near, far = pl.pallas_call(
        hidden_kernel,
        out_shape=[
            jax.ShapeDtypeStruct((rows, width), BF16),
            jax.ShapeDtypeStruct((pack_rows, width), BF16),
            jax.ShapeDtypeStruct((pack_rows, width), BF16),
        ],
        in_specs=[smem, hbm, vmem, vmem],
        out_specs=[vmem, vmem, vmem],
        scratch_shapes=[
            pltpu.VMEM((rows, width), BF16),
            pltpu.SemaphoreType.DMA((blocks,)),
        ],
        compiler_params=pltpu.CompilerParams(vmem_limit_bytes=8 * 2**20),
        name="hidden_and_packs",
    )(*in_hbm(noise_level, frames, mod_table, context))

    same_chip = [(i, i ^ 1) for i in range(devices) if i ^ 1 < devices]
    across = [(i, i + 1) for i in range(1, devices - 1, 2)]
    across += [(b, a) for a, b in across]
    far_got = lax.ppermute(far, "seq", across)
    near_got = lax.ppermute(near, "seq", same_chip)

    open_rows = WMAX * BLK
    scalar_scratch = [
        pltpu.SMEM(band_width.shape, jnp.int32),
        pltpu.SMEM(banded_attender_factor.shape, F32),
        pltpu.SMEM(cross_temp.shape, F32),
        pltpu.SMEM(alignment.shape[::-1], jnp.int32),
        pltpu.SMEM(counts.shape, jnp.int32),
    ]
    scalars = in_hbm(band_width, banded_attender_factor, cross_temp, alignment.T, counts)
    loads = 3 * qwidth // CHUNK + 4
    update, acc, weight, peaks, q, cq = pl.pallas_call(
        main_kernel,
        out_shape=[
            jax.ShapeDtypeStruct((rows, width), BF16),
            jax.ShapeDtypeStruct((open_rows, qwidth), F32),
            jax.ShapeDtypeStruct((open_rows, qwidth), F32),
            jax.ShapeDtypeStruct((open_rows, LANES), F32),
            jax.ShapeDtypeStruct((rows, qwidth), BF16),
            jax.ShapeDtypeStruct((rows, cqwidth), BF16),
        ],
        in_specs=[hbm] * 5 + [vmem] * 3 + [hbm] * 5,
        out_specs=[hbm] + [vmem] * 5,
        scratch_shapes=scalar_scratch
        + [
            pltpu.VMEM(qkv_weight.shape, BF16),
            pltpu.VMEM(cross_query_weight.shape, BF16),
            pltpu.VMEM(cross_kv_weight.shape, BF16),
            pltpu.VMEM(out_weight.shape, BF16),
            pltpu.VMEM(cross_out_weight.shape, BF16),
            pltpu.VMEM((window, cwidth), BF16),
            pltpu.VMEM((rows + halo, qwidth), BF16),
            pltpu.VMEM((pairs, rows + halo, 2 * LANES), BF16),
            pltpu.VMEM((window, cqwidth), BF16),
            pltpu.VMEM((cross_pairs, window, 2 * LANES), BF16),
            pltpu.VMEM((done * BLK, qwidth), BF16),
            pltpu.VMEM((done * BLK, cqwidth), BF16),
            pltpu.VMEM((done * BLK, width), BF16),
            pltpu.SemaphoreType.DMA((loads + 5,)),
        ],
        compiler_params=pltpu.CompilerParams(vmem_limit_bytes=MAIN_VMEM),
        cost_estimate=pl.CostEstimate(
            flops=12 * 10**9, bytes_accessed=20 * 10**6, transcendentals=5 * 10**6
        ),
        name="local_attention",
    )(
        *scalars,
        hidden,
        near_got,
        *in_hbm(
            context,
            qkv_weight,
            cross_query_weight,
            cross_kv_weight,
            out_weight,
            cross_out_weight,
        ),
    )

    return pl.pallas_call(
        tail_kernel,
        out_shape=jax.ShapeDtypeStruct((rows, width), BF16),
        in_specs=[hbm] * 5 + [vmem] * 12 + [hbm],
        out_specs=hbm,
        scratch_shapes=scalar_scratch
        + [
            pltpu.VMEM((window, cwidth), BF16),
            pltpu.VMEM((halo, qwidth), BF16),
            pltpu.VMEM((pairs, halo, 2 * LANES), BF16),
            pltpu.VMEM((window, cqwidth), BF16),
            pltpu.VMEM((cross_pairs, window, 2 * LANES), BF16),
            pltpu.VMEM((open_rows, qwidth), BF16),
            pltpu.VMEM((open_rows, cqwidth), BF16),
            pltpu.VMEM((open_rows, width), BF16),
            pltpu.SemaphoreType.DMA((WMAX + 5,)),
        ],
        input_output_aliases={17: 0},
        compiler_params=pltpu.CompilerParams(vmem_limit_bytes=TAIL_VMEM),
        cost_estimate=pl.CostEstimate(
            flops=5 * 10**9, bytes_accessed=12 * 10**6, transcendentals=10**6
        ),
        name="halo_attention",
    )(
        *scalars,
        far_got,
        near_got,
        *in_hbm(context),
        qkv_weight,
        cross_kv_weight,
        out_weight,
        cross_out_weight,
        acc,
        weight,
        peaks,
        q,
        cq,
        update,
    )


def solution(mesh):
    placed = (
        P(("groups", "seq"), None),
        P(("groups", "seq"), None),
        P(("groups", "seq")),
        P(("groups", "seq"), None),
        P(("groups", "seq")),
        P(),
        P(),
        P(),
        P(),
        P(),
        P(),
        P(),
        P(),
        P(),
    )
    return jax.shard_map(
        shards, mesh=mesh, in_specs=placed, out_specs=P(("groups", "seq"), None), check_vma=False
    )
```

time: 134 us -> 42.3 us (0.32); the launches traced: 132 us -> 42.1 us
  matrix products: 53.7 us -> 0 us
  local copies, waits for them, and re-layouts: 40.2 us -> 0.03 us
  Pallas kernels: 0 us -> 37.2 us
  other arithmetic: 25.8 us -> 0.01 us
  starting transfers between devices: 12.3 us -> 4.62 us
    pallas_call x0 -> x3, Pallas kernels: none -> 37.2 us  [the longest x1 23 us: shards(): pl.pallas_call(main_kernel, out_shape=[jax.ShapeDtypeStruct((rows, width)...]
    dot_general x9 -> x0, matrix products: 31.9 us -> none  [the longest x1 13.9 us: attend(): jnp.einsum('hij,jhd->ihd', weights, value_rows, preferred_element_type=jn...]
    sub x1 -> x0, matrix products: 21.8 us -> none  [masked_softmax(): powers = jnp.exp(scores - peak)]
    mul x9 -> x0, local copies, waits for them, and re-layouts: 17.8 us -> none  [the longest x6 11 us: head_norm(): parts * lax.rsqrt(jnp.mean(parts * parts, axis=-1, keepdims=True) + 1e-06)]
    slice x7 -> x0, local copies, waits for them, and re-layouts: 15.3 us -> none  [the longest x2 6.37 us: attend(): key_rows = key_pairs[:, :query_width].reshape(-1, BANDED_ATTEND_CT, HD)]
    ppermute x4 -> x2, starting transfers between devices: 12.3 us -> 4.62 us  [the longest x1 4.49 us: shards(): far_got = lax.ppermute(far, 'seq', across)]
    convert_element_type x3 -> x0, other arithmetic: 7.36 us -> none  [the longest x1 5.25 us: shards(): head_norm(projected[:, :query_width], BANDED_ATTEND_CT).astype(jnp.bfloat16)]
    reduce_sum x4 -> x0, other arithmetic: 6.35 us -> none  [the longest x3 4.85 us: head_norm(): jnp.mean(parts * parts, axis=-1, keepdims=True) + 1e-06]
  transfers between devices with their start and end apart: 4 -> 2, of which waited for: 0 -> 0; matrix products, arithmetic and copies ran while one was open for 50% -> 0% of each run, Pallas kernels for 0% -> 55%
where the time goes in v2:
time: 42.3 us; the launch traced here: 42.1 us
  Pallas kernels  37.2 us (88%)
  starting transfers between devices  4.62 us (11%)
    pallas_call x1, Pallas kernels, shards(): pl.pallas_call(main_kernel, out_shape=[jax.ShapeDtypeStruct((rows, width)...  23 us
    pallas_call x1, Pallas kernels, shards(): pl.pallas_call(tail_kernel, out_shape=jax.ShapeDtypeStruct((rows, width),...  11.1 us
    ppermute x1, starting transfers between devices, shards(): far_got = lax.ppermute(far, 'seq', across)  4.49 us
    pallas_call x1, Pallas kernels, shards(): pl.pallas_call(hidden_kernel, out_shape=[jax.ShapeDtypeStruct((rows, widt...  3.09 us
  transfers between devices with their start and end apart: 2, of which 0 were waited for; matrix products, arithmetic and copies ran while one was open for 0% of the time, Pallas kernels for 55%

profile of v2, /device:TPU:1, one launch (start us, length us, event | category | flops | bytes accessed | tf_op | source)
XLA Modules:
  0.0 42.1 jit_solution(11784994146344672925)
XLA Ops:
  0.0 0.0 slice-start
  0.0 3.1 %hidden_and_packs.1 = (bf16[512,1024]{1,0:T(8,128)(2,1)S(1)}, bf16[288,1024]{1,0:T(8,128)(2,1)S(1)}, bf16[288,1024]{1,0:T(8,128)(2,1)S(1)}) custom-call(s32[4]{0:T(128)} %level.1, bf16[512,1024]{1,0:T(8,128)(2,1)} %frames.1, f32[8,2048]{1,0:T(8,128)} %table.1, bf16[96,512]{1,0:T(8,128)(2,1)} %context.5), custom_call_target="tpu_custom_call" | custom-call | tf_op jit(solution)/shard_map/hidden_and_packs/pallas_call | solution.py:628
  3.1 0.1 collective-permute-start.1
  3.2 4.5 %collective-permute-start = (bf16[288,1024]{1,0:T(8,128)(2,1)S(1)}, bf16[288,1024]{1,0:T(8,128)(2,1)S(1)}, u32[]{:S(2)}, u32[]{:S(2)}) collective-permute-start(bf16[288,1024]{1,0:T(8,128)(2,1)S(1)} %get-tuple-element.14), channel_id=1, source_target_pairs={{1,2},{3,4},{5,6},{7,8},{9,10},{11,12},{13,14},{2,1},{4,3},{6,5},{... | collective-permute-start | bytes 1769480 | tf_op jit(solution)/shard_map/ppermute | solution.py:648
  7.7 0.0 collective-permute-done.1.near
  7.7 0.0 slice-start.1
  7.8 0.0 copy-start
  7.8 0.0 copy-start.1
  7.8 0.0 copy-start.2
  7.8 23.0 %local_attention.1 = (bf16[512,1024]{1,0:T(8,128)(2,1)}, f32[256,1024]{1,0:T(8,128)S(1)}, f32[256,1024]{1,0:T(8,128)S(1)}, f32[256,128]{1,0:T(8,128)S(1)}, bf16[...) custom-call(s32[16]{0:T(128)} %band_in.3, f32[16]{0:T(128)} %factor_in.3, f32[8]{0:T(128)} %temp_in.3, ...), custom_call_target="tpu_custom_call" | custom-call | flops 12000000000 | bytes 20000000 | tf_op jit(solution)/shard_map/local_attention/pallas_call | solution.py:661
  30.8 0.0 collective-permute-done.pack
  30.8 0.0 slice-done
  30.8 0.0 slice-done.1
  30.8 0.0 copy-done
  30.8 0.0 copy-done.1
  30.9 0.0 copy-done.2
  30.9 11.1 %halo_attention.1 = bf16[512,1024]{1,0:T(8,128)(2,1)} custom-call(s32[16]{0:T(128)} %band_in.3, f32[16]{0:T(128)} %factor_in.3, f32[8]{0:T(128)} %temp_in.3, s32[2,4]{1,0:T(2,128)} %bitcast.4, s32[4]{0:T(128)} %counts_in.3, bf16[288,1024]{1,0:T(8,128)(2,1)S(1)} %collective-permute-done.pack, ...), custom_call_target="tpu_custom_call", output_to_operand_aliasing={{}: (17, {})} | custom-call | flops 5000000000 | bytes 12000000 | tf_op jit(solution)/shard_map/halo_attention/pallas_call | solution.py:709
  (1 shorter events, 0.0 us)
Async XLA Ops:
  0.0 30.8 %slice-start = ((s8[6291456]{0:T(1024)(128)(4,1)}), s8[4194304]{0:T(1024)(128)(4,1)S(1)}, s32[]{:S(2)}) async-start(s8[6291456]{0:T(1024)(128)(4,1)} %bitcast.1), calls=%async_computation | async-start | bytes 8388608
  3.1 4.6 %collective-permute-start.1 = (bf16[288,1024]{1,0:T(8,128)(2,1)S(1)}, bf16[288,1024]{1,0:T(8,128)(2,1)S(1)}, u32[]{:S(2)}, u32[]{:S(2)}) collective-permute-start(bf16[288,1024]{1,0:T(8,128)(2,1)S(1)} %get-tuple-element.15), channel_id=1, source_target_pairs={{0,1},{1,0},{2,3},{3,2},{4,5},{5,4},{6,7},{7,6},{8,9},{9,8},{10,11... | collective-permute-start | bytes 1769480 | tf_op jit(solution)/shard_map/ppermute | solution.py:649
  3.2 27.6 %collective-permute-start = (bf16[288,1024]{1,0:T(8,128)(2,1)S(1)}, bf16[288,1024]{1,0:T(8,128)(2,1)S(1)}, u32[]{:S(2)}, u32[]{:S(2)}) collective-permute-start(bf16[288,1024]{1,0:T(8,128)(2,1)S(1)} %get-tuple-element.14), channel_id=1, source_target_pairs={{1,2},{3,4},{5,6},{7,8},{9,10},{11,12},{13,14},{2,1},{4,3},{6,5},{... | collective-permute-start | bytes 1769480 | tf_op jit(solution)/shard_map/ppermute | solution.py:648
  7.7 23.1 %slice-start.1 = ((s8[6291456]{0:T(1024)(128)(4,1)}), s8[2097152]{0:T(1024)(128)(4,1)S(1)}, s32[]{:S(2)}) async-start(s8[6291456]{0:T(1024)(128)(4,1)} %bitcast.1), calls=%async_computation.1 | async-start | bytes 4194304
  7.8 23.1 %copy-start = (bf16[1024,1024]{1,0:T(8,128)(2,1)S(1)}, bf16[1024,1024]{1,0:T(8,128)(2,1)}, u32[]{:S(2)}) copy-start(bf16[1024,1024]{1,0:T(8,128)(2,1)} %wo.1) | copy-start | bytes 6291460
  7.8 23.1 %copy-start.1 = (bf16[512,1024]{1,0:T(8,128)(2,1)S(1)}, bf16[512,1024]{1,0:T(8,128)(2,1)}, u32[]{:S(2)}) copy-start(bf16[512,1024]{1,0:T(8,128)(2,1)} %wckv.1) | copy-start | bytes 3145732
  7.8 23.1 %copy-start.2 = (bf16[512,1024]{1,0:T(8,128)(2,1)S(1)}, bf16[512,1024]{1,0:T(8,128)(2,1)}, u32[]{:S(2)}) copy-start(bf16[512,1024]{1,0:T(8,128)(2,1)} %wco.1) | copy-start | bytes 3145732

commit v3 on v2

--- a/solution.py
+++ b/solution.py
@@ -23,7 +23,7 @@
 PLAIN_FACTOR = 8.0
 F32 = jnp.float32
 BF16 = jnp.bfloat16
-MAIN_VMEM = 32 * 2**20
+MAIN_VMEM = 24 * 2**20
 TAIL_VMEM = 16 * 2**20
 TOK_PACK = 32
 
@@ -134,22 +134,46 @@
     return pl.ds(pl.multiple_of(pair * LANES, LANES), LANES)
 
 
-def hidden_kernel(level, frames, table, context, hidden, near, far, stage, sems):
+def hidden_kernel(
+    level_in,
+    frames,
+    table_in,
+    context_in,
+    wqkv,
+    hidden,
+    near,
+    far,
+    context,
+    wqk,
+    level,
+    table,
+    stage,
+    sems,
+):
     odd = lax.rem(lax.axis_index("seq"), 2) == 1
     rows, width = frames.shape
     blocks = rows // BLK
-    copies = []
-    for b in range(blocks):
-        at = pl.ds(b * BLK, BLK)
-        copies.append(pltpu.make_async_copy(frames.at[at], stage.at[at], sems.at[b]))
-        copies[-1].start()
+    loads = [(level_in, level), (table_in, table)]
+    loads += [
+        (frames.at[pl.ds(b * BLK, BLK)], stage.at[pl.ds(b * BLK, BLK)]) for b in range(blocks)
+    ]
+    loads.append((context_in, context))
+    for start in range(0, wqk.shape[1], CHUNK):
+        cols = pl.ds(start, CHUNK)
+        loads.append((wqkv.at[:, cols], wqk.at[:, cols]))
+    loads = [pltpu.make_async_copy(a, b, sems.at[i]) for i, (a, b) in enumerate(loads)]
+    for load in loads:
+        load.start()
+    loads[0].wait()
+    loads[1].wait()
     for b in range(blocks):
         at = pl.ds(b * BLK, BLK)
         row = table[pl.ds(level[b], 1), :]
-        copies[b].wait()
+        loads[2 + b].wait()
         x = stage[at, :].astype(F32)
         x = x * lax.rsqrt(jnp.mean(x * x, axis=1, keepdims=True) + 1e-06)
         hidden[at, :] = (x * (1.0 + row[:, :width]) + row[:, width:]).astype(BF16)
+    loads[2 + blocks].wait()
     halo = WMAX * BLK
     tokens = context.shape[0]
     cwidth = context.shape[1]
@@ -161,6 +185,8 @@
         pack[halo:, :cwidth] = tok[:TOK_PACK]
         pack[halo : halo + 16, cwidth:] = tok[TOK_PACK:]
         pack[halo + 16 :, cwidth:] = jnp.zeros((TOK_PACK - 16, cwidth), BF16)
+    for load in loads[3 + blocks :]:
+        load.wait()
 
 
 def unpack_tokens(pack, halo, cwidth):
@@ -201,8 +227,7 @@
             pltpu.make_async_copy(stage.at[at], out.at[pl.ds(to, BLK)], sems.at[i])
         )
         copies[-1].start()
-    for copy in copies:
-        copy.wait()
+    return copies
 
 
 def main_kernel(
@@ -214,6 +239,7 @@
     hidden,
     near,
     context,
+    wqk,
     wqkv_in,
     wcq_in,
     wckv_in,
@@ -225,16 +251,16 @@
     peak_out,
     q,
     cq,
+    wv,
+    wckv,
+    wo,
+    wco,
     band,
     factor,
     temp,
     align,
     counts,
-    wqkv,
     wcq,
-    wckv,
-    wo,
-    wco,
     tokens,
     keys,
     vext,
@@ -257,20 +283,19 @@
     other = jnp.where(odd, 0, rows)
 
     loads = []
-    for start in range(0, 3 * qwidth, CHUNK):
-        cols = pl.ds(start, CHUNK)
-        loads.append((wqkv_in.at[:, cols], wqkv.at[:, cols]))
+    for start in range(0, qwidth, CHUNK):
+        loads.append(
+            (wqkv_in.at[:, pl.ds(2 * qwidth + start, CHUNK)], wv.at[:, pl.ds(start, CHUNK)])
+        )
     loads += [(wcq_in, wcq), (wckv_in, wckv), (wo_in, wo), (wco_in, wco)]
     loads = [pltpu.make_async_copy(a, b, sems.at[i]) for i, (a, b) in enumerate(loads)]
-    for load in loads[:2]:
-        load.start()
     scalars = scalar_copies(
         (band_in, factor_in, temp_in, align_in, counts_in),
         (band, factor, temp, align, counts),
         sems,
         len(loads),
     )
-    for load in loads[2:]:
+    for load in loads:
         load.start()
 
     vext[:, :, LANES:] = jnp.ones((vext.shape[0], vext.shape[1], LANES), BF16)
@@ -282,7 +307,10 @@
 
     def project(source, first, to, start):
         def begin():
-            return dot(source[first : first + TILE, :], wqkv[:, start : start + CHUNK])
+            part, col = divmod(start, qwidth)
+            weight = wv if part == 2 else wqk
+            col = col if part == 2 else start
+            return dot(source[first : first + TILE, :], weight[:, col : col + CHUNK])
 
         def end(x):
             at = pl.ds(pl.multiple_of(to + first, BLK), TILE)
@@ -306,15 +334,17 @@
         return begin, end
 
     items = []
-    for i, start in enumerate(range(0, 3 * qwidth, CHUNK)):
+    for start in range(0, 3 * qwidth, CHUNK):
         tiles = [project(hidden, first, own, start) for first in range(0, rows, TILE)]
         if start >= qwidth:
             tiles += [project(near, first, other, start) for first in range(0, halo, TILE)]
-        begin, end = tiles[0]
-        tiles[0] = (lambda i=i, begin=begin: (loads[i].wait(), begin())[1], end)
+        if start >= 2 * qwidth:
+            load = loads[(start - 2 * qwidth) // CHUNK]
+            begin, end = tiles[0]
+            tiles[0] = (lambda load=load, begin=begin: (load.wait(), begin())[1], end)
         items += tiles
     staggered(items)
-    count = 3 * qwidth // CHUNK
+    count = qwidth // CHUNK
     loads[count].wait()
     loads[count + 1].wait()
     staggered([project_cross(first) for first in range(0, rows, TILE)])
@@ -391,11 +421,23 @@
     pairs, cross_pairs = qwidth // LANES, cwidth // LANES
     easy = plain(factor, temp)
 
+    def project_out():
+        for load in loads[count + 2 :]:
+            load.wait()
+        total = dot(mine[...], wo[...]) + dot(cross_mine[...], wco[...])
+        return finish(total, out, stage, sems, 0, done, odd, blocks)
+
     @pl.when(easy)
     def _():
         items = [cross_item(p, f, False) for p in range(cross_pairs) for f in range(done)]
-        items += [self_item(p, f, False) for p in range(pairs) for f in range(blocks)]
+        items += [self_item(p, f, False) for p in range(pairs) for f in range(done)]
         staggered(items)
+        copies = project_out()
+        staggered(
+            [self_item(p, f, False) for p in range(pairs) for f in range(done, blocks)]
+        )
+        for copy in copies:
+            copy.wait()
 
     @pl.when(jnp.logical_not(easy))
     def _():
@@ -409,10 +451,8 @@
         def _(p):
             staggered([cross_item(p, f, True) for f in range(done)])
 
-    for load in loads[count + 2 :]:
-        load.wait()
-    total = dot(mine[...], wo[...]) + dot(cross_mine[...], wco[...])
-    finish(total, out, stage, sems, 0, done, odd, blocks)
+        for copy in project_out():
+            copy.wait()
 
 
 def tail_kernel(
@@ -424,7 +464,8 @@
     pack,
     near,
     context,
-    wqkv,
+    wqk,
+    wv,
     wckv,
     wo,
     wco,
@@ -477,7 +518,10 @@
 
     def project(first, start):
         def begin():
-            return dot(pack[first : first + TILE, :], wqkv[:, start : start + CHUNK])
+            part, col = divmod(start, qwidth)
+            weight = wv if part == 2 else wqk
+            col = col if part == 2 else start
+            return dot(pack[first : first + TILE, :], weight[:, col : col + CHUNK])
 
         def end(x):
             part, col = divmod(start, qwidth)
@@ -591,7 +635,8 @@
             staggered([cross_item(p, f, True) for f in range(done, blocks)])
 
     total = dot(mine[...], wo[...]) + dot(cross_mine[...], wco[...])
-    finish(total, out, stage, sems, done, WMAX, odd, blocks)
+    for copy in finish(total, out, stage, sems, done, WMAX, odd, blocks):
+        copy.wait()
 
 
 def shards(
@@ -620,27 +665,30 @@
     pairs, cross_pairs = qwidth // LANES, cqwidth // LANES
     window = tokens + 2 * RCH * TOKB
     devices = lax.axis_size("seq")
-    smem = pl.BlockSpec(memory_space=pltpu.SMEM)
     vmem = pl.BlockSpec(memory_space=pltpu.VMEM)
     hbm = pl.BlockSpec(memory_space=pltpu.HBM)
     pack_rows = halo + TOK_PACK
 
-    hidden, near, far = pl.pallas_call(
+    hidden, near, far, context, wqk = pl.pallas_call(
         hidden_kernel,
         out_shape=[
             jax.ShapeDtypeStruct((rows, width), BF16),
             jax.ShapeDtypeStruct((pack_rows, width), BF16),
             jax.ShapeDtypeStruct((pack_rows, width), BF16),
+            jax.ShapeDtypeStruct(context.shape, BF16),
+            jax.ShapeDtypeStruct((width, 2 * qwidth), BF16),
         ],
-        in_specs=[smem, hbm, vmem, vmem],
-        out_specs=[vmem, vmem, vmem],
+        in_specs=[hbm] * 5,
+        out_specs=[vmem] * 5,
         scratch_shapes=[
+            pltpu.SMEM(noise_level.shape, jnp.int32),
+            pltpu.VMEM(mod_table.shape, F32),
             pltpu.VMEM((rows, width), BF16),
-            pltpu.SemaphoreType.DMA((blocks,)),
+            pltpu.SemaphoreType.DMA((blocks + 3 + 2 * qwidth // CHUNK,)),
         ],
         compiler_params=pltpu.CompilerParams(vmem_limit_bytes=8 * 2**20),
         name="hidden_and_packs",
-    )(*in_hbm(noise_level, frames, mod_table, context))
+    )(*in_hbm(noise_level, frames, mod_table, context, qkv_weight))
 
     same_chip = [(i, i ^ 1) for i in range(devices) if i ^ 1 < devices]
     across = [(i, i + 1) for i in range(1, devices - 1, 2)]
@@ -657,8 +705,8 @@
         pltpu.SMEM(counts.shape, jnp.int32),
     ]
     scalars = in_hbm(band_width, banded_attender_factor, cross_temp, alignment.T, counts)
-    loads = 3 * qwidth // CHUNK + 4
-    update, acc, weight, peaks, q, cq = pl.pallas_call(
+    loads = qwidth // CHUNK + 4
+    update, acc, weight, peaks, q, cq, wv, wckv, wo, wco = pl.pallas_call(
         main_kernel,
         out_shape=[
             jax.ShapeDtypeStruct((rows, width), BF16),
@@ -667,16 +715,16 @@
             jax.ShapeDtypeStruct((open_rows, LANES), F32),
             jax.ShapeDtypeStruct((rows, qwidth), BF16),
             jax.ShapeDtypeStruct((rows, cqwidth), BF16),
+            jax.ShapeDtypeStruct((width, qwidth), BF16),
+            jax.ShapeDtypeStruct(cross_kv_weight.shape, BF16),
+            jax.ShapeDtypeStruct(out_weight.shape, BF16),
+            jax.ShapeDtypeStruct(cross_out_weight.shape, BF16),
         ],
-        in_specs=[hbm] * 5 + [vmem] * 3 + [hbm] * 5,
-        out_specs=[hbm] + [vmem] * 5,
+        in_specs=[hbm] * 5 + [vmem] * 4 + [hbm] * 5,
+        out_specs=[hbm] + [vmem] * 9,
         scratch_shapes=scalar_scratch
         + [
-            pltpu.VMEM(qkv_weight.shape, BF16),
             pltpu.VMEM(cross_query_weight.shape, BF16),
-            pltpu.VMEM(cross_kv_weight.shape, BF16),
-            pltpu.VMEM(out_weight.shape, BF16),
-            pltpu.VMEM(cross_out_weight.shape, BF16),
             pltpu.VMEM((window, cwidth), BF16),
             pltpu.VMEM((rows + halo, qwidth), BF16),
             pltpu.VMEM((pairs, rows + halo, 2 * LANES), BF16),
@@ -696,8 +744,9 @@
         *scalars,
         hidden,
         near_got,
+        context,
+        wqk,
         *in_hbm(
-            context,
             qkv_weight,
             cross_query_weight,
             cross_kv_weight,
@@ -709,7 +758,7 @@
     return pl.pallas_call(
         tail_kernel,
         out_shape=jax.ShapeDtypeStruct((rows, width), BF16),
-        in_specs=[hbm] * 5 + [vmem] * 12 + [hbm],
+        in_specs=[hbm] * 5 + [vmem] * 13 + [hbm],
         out_specs=hbm,
         scratch_shapes=scalar_scratch
         + [
@@ -723,7 +772,7 @@
             pltpu.VMEM((open_rows, width), BF16),
             pltpu.SemaphoreType.DMA((WMAX + 5,)),
         ],
-        input_output_aliases={17: 0},
+        input_output_aliases={18: 0},
         compiler_params=pltpu.CompilerParams(vmem_limit_bytes=TAIL_VMEM),
         cost_estimate=pl.CostEstimate(
             flops=5 * 10**9, bytes_accessed=12 * 10**6, transcendentals=10**6
@@ -733,11 +782,12 @@
         *scalars,
         far_got,
         near_got,
-        *in_hbm(context),
-        qkv_weight,
-        cross_kv_weight,
-        out_weight,
-        cross_out_weight,
+        context,
+        wqk,
+        wv,
+        wckv,
+        wo,
+        wco,
         acc,
         weight,
         peaks,

time: 42.3 us -> 38.8 us (0.917)
  Pallas kernels: 37.2 us -> 33.8 us
    pallas_call x1, Pallas kernels: 23 us -> 20.9 us  [shards(): pl.pallas_call(main_kernel, out_shape=[jax.ShapeDtypeStruct((rows, width)...]
    pallas_call x1, Pallas kernels: 11.1 us -> 10.2 us  [shards(): pl.pallas_call(tail_kernel, out_shape=jax.ShapeDtypeStruct((rows, width),...]
  transfers between devices with their start and end apart: 2 -> 2, of which waited for: 0 -> 0; matrix products, arithmetic and copies ran while one was open for 0% -> 0% of each run, Pallas kernels for 55% -> 54%
where the time goes in v3:
time: 38.8 us; the launch traced here: 38.6 us
  Pallas kernels  33.8 us (87%)
  starting transfers between devices  4.62 us (12%)
    pallas_call x1, Pallas kernels, shards(): pl.pallas_call(main_kernel, out_shape=[jax.ShapeDtypeStruct((rows, width)...  20.9 us
    pallas_call x1, Pallas kernels, shards(): pl.pallas_call(tail_kernel, out_shape=jax.ShapeDtypeStruct((rows, width),...  10.2 us
    ppermute x1, starting transfers between devices, shards(): far_got = lax.ppermute(far, 'seq', across)  4.49 us
    pallas_call x1, Pallas kernels, shards(): pl.pallas_call(hidden_kernel, out_shape=[jax.ShapeDtypeStruct((rows, widt...  2.68 us
  transfers between devices with their start and end apart: 2, of which 0 were waited for; matrix products, arithmetic and copies ran while one was open for 0% of the time, Pallas kernels for 54%

profile of v3, /device:TPU:1, one launch (start us, length us, event | category | flops | bytes accessed | tf_op | source)
XLA Modules:
  0.0 38.6 jit_solution(6120707456445677862)
XLA Ops:
  0.0 2.7 %hidden_and_packs.1 = (bf16[512,1024]{1,0:T(8,128)(2,1)S(1)}, bf16[288,1024]{1,0:T(8,128)(2,1)S(1)}, bf16[288,1024]{1,0:T(8,128)(2,1)S(1)}, bf16[96,512]{1,0:T(8,128)(2,1)S(1)}, bf16[1024,2048]{1,0:T(8,128)(2,1)S(1)}) custom-call(s32[4]{0:T(128)} %level_in.1, bf16[512,1024]{1,0:T(8,128)(2,1)} %frames.1, f32[8,2048]{1,0:T(8,128)} %table_in.1, ...), custom_call_target="tpu_custom_call" | custom-call | tf_op jit(solution)/shard_map/hidden_and_packs/pallas_call | solution.py:672
  2.7 0.1 collective-permute-start.1
  2.8 4.5 %collective-permute-start = (bf16[288,1024]{1,0:T(8,128)(2,1)S(1)}, bf16[288,1024]{1,0:T(8,128)(2,1)S(1)}, u32[]{:S(2)}, u32[]{:S(2)}) collective-permute-start(bf16[288,1024]{1,0:T(8,128)(2,1)S(1)} %get-tuple-element.20), channel_id=1, source_target_pairs={{1,2},{3,4},{5,6},{7,8},{9,10},{11,12},{13,14},{2,1},{4,3},{6,5},{... | collective-permute-start | bytes 1769480 | tf_op jit(solution)/shard_map/ppermute | solution.py:696
  7.3 0.0 collective-permute-done.1.near
  7.3 20.9 %local_attention.1 = (bf16[512,1024]{1,0:T(8,128)(2,1)}, f32[256,1024]{1,0:T(8,128)S(1)}, f32[256,1024]{1,0:T(8,128)S(1)}, f32[256,128]{1,0:T(8,128)S(1)}, bf16[...) custom-call(s32[16]{0:T(128)} %band_in.3, ...), custom_call_target="tpu_custom_call" | custom-call | flops 12000000000 | bytes 20000000 | tf_op jit(solution)/shard_map/local_attention/pallas_call | solution.py:709
  28.2 0.0 collective-permute-done.pack
  28.2 10.2 %halo_attention.1 = bf16[512,1024]{1,0:T(8,128)(2,1)} custom-call(s32[16]{0:T(128)} %band_in.3, f32[16]{0:T(128)} %factor_in.3, f32[8]{0:T(128)} %temp_in.3, s32[2,4]{1,0:T(2,128)} %bitcast.2, s32[4]{0:T(128)} %counts_in.3, bf16[288,1024]{1,0:T(8,128)(2,1)S(1)} %collective-permute-done.pack, ...), custom_call_target="tpu_custom_call", output_to_operand_aliasing={{}: (18, {})} | custom-call | flops 5000000000 | bytes 12000000 | tf_op jit(solution)/shard_map/halo_attention/pallas_call | solution.py:758
Async XLA Ops:
  2.7 4.6 %collective-permute-start.1 = (bf16[288,1024]{1,0:T(8,128)(2,1)S(1)}, bf16[288,1024]{1,0:T(8,128)(2,1)S(1)}, u32[]{:S(2)}, u32[]{:S(2)}) collective-permute-start(bf16[288,1024]{1,0:T(8,128)(2,1)S(1)} %get-tuple-element.21), channel_id=1, source_target_pairs={{0,1},{1,0},{2,3},{3,2},{4,5},{5,4},{6,7},{7,6},{8,9},{9,8},{10,11... | collective-permute-start | bytes 1769480 | tf_op jit(solution)/shard_map/ppermute | solution.py:697
  2.8 25.4 %collective-permute-start = (bf16[288,1024]{1,0:T(8,128)(2,1)S(1)}, bf16[288,1024]{1,0:T(8,128)(2,1)S(1)}, u32[]{:S(2)}, u32[]{:S(2)}) collective-permute-start(bf16[288,1024]{1,0:T(8,128)(2,1)S(1)} %get-tuple-element.20), channel_id=1, source_target_pairs={{1,2},{3,4},{5,6},{7,8},{9,10},{11,12},{13,14},{2,1},{4,3},{6,5},{... | collective-permute-start | bytes 1769480 | tf_op jit(solution)/shard_map/ppermute | solution.py:696

commit v4 on v3

--- a/solution.py
+++ b/solution.py
@@ -139,12 +139,10 @@
     frames,
     table_in,
     context_in,
-    wqkv,
     hidden,
     near,
     far,
     context,
-    wqk,
     level,
     table,
     stage,
@@ -158,9 +156,6 @@
         (frames.at[pl.ds(b * BLK, BLK)], stage.at[pl.ds(b * BLK, BLK)]) for b in range(blocks)
     ]
     loads.append((context_in, context))
-    for start in range(0, wqk.shape[1], CHUNK):
-        cols = pl.ds(start, CHUNK)
-        loads.append((wqkv.at[:, cols], wqk.at[:, cols]))
     loads = [pltpu.make_async_copy(a, b, sems.at[i]) for i, (a, b) in enumerate(loads)]
     for load in loads:
         load.start()
@@ -195,13 +190,18 @@
     )
 
 
-def token_pairs(tokens, wckv, ck, cvext):
+def token_item(rows, start, wckv, ck, cvext):
+    at = pl.ds(start, rows.shape[0])
     cwidth = ck.shape[1]
-    x = tokens[...]
-    ck[...] = head_norm(dot(x, wckv[:, :cwidth]))
-    values = dot(x, wckv[:, cwidth:]).astype(BF16)
-    for pair in range(cwidth // LANES):
-        cvext[pair, :, :LANES] = values[:, lanes_of(pair)]
+
+    def begin():
+        return dot(rows[...], wckv[...])
+
+    def end(x):
+        ck[at, :] = head_norm(x[:, :cwidth])
+        store_values(cvext, at, 0, x[:, cwidth:].astype(BF16))
+
+    return begin, end
 
 
 def store_values(vext, at, start, values):
@@ -239,10 +239,9 @@
     hidden,
     near,
     context,
-    wqk,
-    wqkv_in,
-    wcq_in,
-    wckv_in,
+    wqkv,
+    wcq,
+    wckv,
     wo_in,
     wco_in,
     out,
@@ -251,21 +250,18 @@
     peak_out,
     q,
     cq,
-    wv,
-    wckv,
     wo,
     wco,
+    ck,
+    cvext,
     band,
     factor,
     temp,
     align,
     counts,
-    wcq,
     tokens,
     keys,
     vext,
-    ck,
-    cvext,
     mine,
     cross_mine,
     stage,
@@ -282,12 +278,7 @@
     own = jnp.where(odd, halo, 0)
     other = jnp.where(odd, 0, rows)
 
-    loads = []
-    for start in range(0, qwidth, CHUNK):
-        loads.append(
-            (wqkv_in.at[:, pl.ds(2 * qwidth + start, CHUNK)], wv.at[:, pl.ds(start, CHUNK)])
-        )
-    loads += [(wcq_in, wcq), (wckv_in, wckv), (wo_in, wo), (wco_in, wco)]
+    loads = [(wo_in, wo), (wco_in, wco)]
     loads = [pltpu.make_async_copy(a, b, sems.at[i]) for i, (a, b) in enumerate(loads)]
     scalars = scalar_copies(
         (band_in, factor_in, temp_in, align_in, counts_in),
@@ -307,10 +298,7 @@
 
     def project(source, first, to, start):
         def begin():
-            part, col = divmod(start, qwidth)
-            weight = wv if part == 2 else wqk
-            col = col if part == 2 else start
-            return dot(source[first : first + TILE, :], weight[:, col : col + CHUNK])
+            return dot(source[first : first + TILE, :], wqkv[:, start : start + CHUNK])
 
         def end(x):
             at = pl.ds(pl.multiple_of(to + first, BLK), TILE)
@@ -338,17 +326,10 @@
         tiles = [project(hidden, first, own, start) for first in range(0, rows, TILE)]
         if start >= qwidth:
             tiles += [project(near, first, other, start) for first in range(0, halo, TILE)]
-        if start >= 2 * qwidth:
-            load = loads[(start - 2 * qwidth) // CHUNK]
-            begin, end = tiles[0]
-            tiles[0] = (lambda load=load, begin=begin: (load.wait(), begin())[1], end)
         items += tiles
+    items += [project_cross(first) for first in range(0, rows, TILE)]
+    items.append(token_item(tokens, 0, wckv, ck, cvext))
     staggered(items)
-    count = qwidth // CHUNK
-    loads[count].wait()
-    loads[count + 1].wait()
-    staggered([project_cross(first) for first in range(0, rows, TILE)])
-    token_pairs(tokens, wckv, ck, cvext)
     for copy in scalars:
         copy.wait()
 
@@ -422,7 +403,7 @@
     easy = plain(factor, temp)
 
     def project_out():
-        for load in loads[count + 2 :]:
+        for load in loads:
             load.wait()
         total = dot(mine[...], wo[...]) + dot(cross_mine[...], wco[...])
         return finish(total, out, stage, sems, 0, done, odd, blocks)
@@ -462,13 +443,12 @@
     align_in,
     counts_in,
     pack,
-    near,
-    context,
-    wqk,
-    wv,
-    wckv,
+    wqkv,
     wo,
     wco,
+    wckv,
+    ck_in,
+    cvext_in,
     acc_in,
     sum_in,
     peak_in,
@@ -481,7 +461,7 @@
     temp,
     align,
     counts,
-    tokens,
+    late,
     keys,
     vext,
     ck,
@@ -499,8 +479,8 @@
     blocks = rows // BLK
     halo = WMAX * BLK
     done = blocks - WMAX
-    cwidth = context.shape[1]
-    window = tokens.shape[0]
+    window, cwidth = ck.shape
+    tokens = window - 2 * RCH * TOKB
 
     scalars = scalar_copies(
         (band_in, factor_in, temp_in, align_in, counts_in),
@@ -509,19 +489,14 @@
         WMAX,
     )
     vext[:, :, LANES:] = jnp.ones((vext.shape[0], vext.shape[1], LANES), BF16)
-    cvext[:, :, LANES:] = jnp.ones((cvext.shape[0], cvext.shape[1], LANES), BF16)
-    tokens[RCH * TOKB : RCH * TOKB + context.shape[0], :] = context[...]
-    ends = [jnp.where(odd, 0, window - RCH * TOKB), jnp.where(odd, window - RCH * TOKB, 0)]
-    for start, source in zip(ends, (near, pack)):
-        at = pl.ds(pl.multiple_of(start, 16), RCH * TOKB)
-        tokens[at, :] = unpack_tokens(source, halo, cwidth)
+    ck[...] = ck_in[...]
+    cvext[...] = cvext_in[...]
+    late[...] = unpack_tokens(pack, halo, wckv.shape[0])
+    late_at = pl.multiple_of(jnp.where(odd, window - RCH * TOKB, 0), 16)
 
     def project(first, start):
         def begin():
-            part, col = divmod(start, qwidth)
-            weight = wv if part == 2 else wqk
-            col = col if part == 2 else start
-            return dot(pack[first : first + TILE, :], weight[:, col : col + CHUNK])
+            return dot(pack[first : first + TILE, :], wqkv[:, start : start + CHUNK])
 
         def end(x):
             part, col = divmod(start, qwidth)
@@ -533,14 +508,13 @@
 
         return begin, end
 
-    staggered(
-        [
-            project(first, start)
-            for start in range(qwidth, 3 * qwidth, CHUNK)
-            for first in range(0, halo, TILE)
-        ]
-    )
-    token_pairs(tokens, wckv, ck, cvext)
+    items = [token_item(late, late_at, wckv, ck, cvext)]
+    items += [
+        project(first, start)
+        for start in range(qwidth, 3 * qwidth, CHUNK)
+        for first in range(0, halo, TILE)
+    ]
+    staggered(items)
     for copy in scalars:
         copy.wait()
 
@@ -590,7 +564,7 @@
             align,
             counts,
             local_block(f, odd, blocks),
-            device * (context.shape[0] // TOKB) - RCH,
+            device * (tokens // TOKB) - RCH,
             window,
         )
         for f in range(done, blocks)
@@ -669,32 +643,32 @@
     hbm = pl.BlockSpec(memory_space=pltpu.HBM)
     pack_rows = halo + TOK_PACK
 
-    hidden, near, far, context, wqk = pl.pallas_call(
+    hidden, near, far, context = pl.pallas_call(
         hidden_kernel,
         out_shape=[
             jax.ShapeDtypeStruct((rows, width), BF16),
             jax.ShapeDtypeStruct((pack_rows, width), BF16),
             jax.ShapeDtypeStruct((pack_rows, width), BF16),
             jax.ShapeDtypeStruct(context.shape, BF16),
-            jax.ShapeDtypeStruct((width, 2 * qwidth), BF16),
         ],
-        in_specs=[hbm] * 5,
-        out_specs=[vmem] * 5,
+        in_specs=[hbm] * 4,
+        out_specs=[vmem] * 4,
         scratch_shapes=[
             pltpu.SMEM(noise_level.shape, jnp.int32),
             pltpu.VMEM(mod_table.shape, F32),
             pltpu.VMEM((rows, width), BF16),
-            pltpu.SemaphoreType.DMA((blocks + 3 + 2 * qwidth // CHUNK,)),
+            pltpu.SemaphoreType.DMA((blocks + 4,)),
         ],
         compiler_params=pltpu.CompilerParams(vmem_limit_bytes=8 * 2**20),
+        cost_estimate=pl.CostEstimate(flops=8 * 10**9, bytes_accessed=4 * 10**6, transcendentals=0),
         name="hidden_and_packs",
-    )(*in_hbm(noise_level, frames, mod_table, context, qkv_weight))
+    )(*in_hbm(noise_level, frames, mod_table, context))
 
     same_chip = [(i, i ^ 1) for i in range(devices) if i ^ 1 < devices]
     across = [(i, i + 1) for i in range(1, devices - 1, 2)]
     across += [(b, a) for a, b in across]
+    near_got = lax.ppermute(near, "seq", same_chip)
     far_got = lax.ppermute(far, "seq", across)
-    near_got = lax.ppermute(near, "seq", same_chip)
 
     open_rows = WMAX * BLK
     scalar_scratch = [
@@ -705,8 +679,8 @@
         pltpu.SMEM(counts.shape, jnp.int32),
     ]
     scalars = in_hbm(band_width, banded_attender_factor, cross_temp, alignment.T, counts)
-    loads = qwidth // CHUNK + 4
-    update, acc, weight, peaks, q, cq, wv, wckv, wo, wco = pl.pallas_call(
+    loads = 2
+    update, acc, weight, peaks, q, cq, wo, wco, ck, cvext = pl.pallas_call(
         main_kernel,
         out_shape=[
             jax.ShapeDtypeStruct((rows, width), BF16),
@@ -715,21 +689,18 @@
             jax.ShapeDtypeStruct((open_rows, LANES), F32),
             jax.ShapeDtypeStruct((rows, qwidth), BF16),
             jax.ShapeDtypeStruct((rows, cqwidth), BF16),
-            jax.ShapeDtypeStruct((width, qwidth), BF16),
-            jax.ShapeDtypeStruct(cross_kv_weight.shape, BF16),
             jax.ShapeDtypeStruct(out_weight.shape, BF16),
             jax.ShapeDtypeStruct(cross_out_weight.shape, BF16),
+            jax.ShapeDtypeStruct((window, cqwidth), BF16),
+            jax.ShapeDtypeStruct((cross_pairs, window, 2 * LANES), BF16),
         ],
-        in_specs=[hbm] * 5 + [vmem] * 4 + [hbm] * 5,
+        in_specs=[hbm] * 5 + [vmem] * 6 + [hbm] * 2,
         out_specs=[hbm] + [vmem] * 9,
         scratch_shapes=scalar_scratch
         + [
-            pltpu.VMEM(cross_query_weight.shape, BF16),
             pltpu.VMEM((window, cwidth), BF16),
             pltpu.VMEM((rows + halo, qwidth), BF16),
             pltpu.VMEM((pairs, rows + halo, 2 * LANES), BF16),
-            pltpu.VMEM((window, cqwidth), BF16),
-            pltpu.VMEM((cross_pairs, window, 2 * LANES), BF16),
             pltpu.VMEM((done * BLK, qwidth), BF16),
             pltpu.VMEM((done * BLK, cqwidth), BF16),
             pltpu.VMEM((done * BLK, width), BF16),
@@ -745,24 +716,20 @@
         hidden,
         near_got,
         context,
-        wqk,
-        *in_hbm(
-            qkv_weight,
-            cross_query_weight,
-            cross_kv_weight,
-            out_weight,
-            cross_out_weight,
-        ),
+        qkv_weight,
+        cross_query_weight,
+        cross_kv_weight,
+        *in_hbm(out_weight, cross_out_weight),
     )
 
     return pl.pallas_call(
         tail_kernel,
         out_shape=jax.ShapeDtypeStruct((rows, width), BF16),
-        in_specs=[hbm] * 5 + [vmem] * 13 + [hbm],
+        in_specs=[hbm] * 5 + [vmem] * 12 + [hbm],
         out_specs=hbm,
         scratch_shapes=scalar_scratch
         + [
-            pltpu.VMEM((window, cwidth), BF16),
+            pltpu.VMEM((RCH * TOKB, cwidth), BF16),
             pltpu.VMEM((halo, qwidth), BF16),
             pltpu.VMEM((pairs, halo, 2 * LANES), BF16),
             pltpu.VMEM((window, cqwidth), BF16),
@@ -772,7 +739,7 @@
             pltpu.VMEM((open_rows, width), BF16),
             pltpu.SemaphoreType.DMA((WMAX + 5,)),
         ],
-        input_output_aliases={18: 0},
+        input_output_aliases={17: 0},
         compiler_params=pltpu.CompilerParams(vmem_limit_bytes=TAIL_VMEM),
         cost_estimate=pl.CostEstimate(
             flops=5 * 10**9, bytes_accessed=12 * 10**6, transcendentals=10**6
@@ -781,13 +748,12 @@
     )(
         *scalars,
         far_got,
-        near_got,
-        context,
-        wqk,
-        wv,
-        wckv,
+        qkv_weight,
         wo,
         wco,
+        cross_kv_weight,
+        ck,
+        cvext,
         acc,
         weight,
         peaks,

time: 38.8 us -> 36.2 us (0.933)
  Pallas kernels: 33.8 us -> 31 us
    pallas_call x1, Pallas kernels: 20.9 us -> 19.5 us  [shards(): pl.pallas_call(main_kernel, out_shape=[jax.ShapeDtypeStruct((rows, width)...]
    pallas_call x1, Pallas kernels: 2.68 us -> 1.96 us  [shards(): pl.pallas_call(hidden_kernel, out_shape=[jax.ShapeDtypeStruct((rows, widt...]
    pallas_call x1, Pallas kernels: 10.2 us -> 9.59 us  [shards(): pl.pallas_call(tail_kernel, out_shape=jax.ShapeDtypeStruct((rows, width),...]
where the time goes in v4:
time: 36.2 us; the launch traced here: 36 us
  Pallas kernels  31 us (86%)
  starting transfers between devices  4.75 us (13%)
    pallas_call x1, Pallas kernels, shards(): pl.pallas_call(main_kernel, out_shape=[jax.ShapeDtypeStruct((rows, width)...  19.5 us
    pallas_call x1, Pallas kernels, shards(): pl.pallas_call(tail_kernel, out_shape=jax.ShapeDtypeStruct((rows, width),...  9.59 us
    ppermute x1, starting transfers between devices, shards(): far_got = lax.ppermute(far, 'seq', across)  4.63 us
    pallas_call x1, Pallas kernels, shards(): pl.pallas_call(hidden_kernel, out_shape=[jax.ShapeDtypeStruct((rows, widt...  1.96 us
  transfers between devices with their start and end apart: 2, of which 0 were waited for; matrix products, arithmetic and copies ran while one was open for 0% of the time, Pallas kernels for 54%

profile of v4, /device:TPU:1, one launch (start us, length us, event | category | flops | bytes accessed | tf_op | source)
XLA Modules:
  0.0 36.0 jit_solution(7362437540178994631)
XLA Ops:
  0.0 0.0 copy-start.2
  0.0 0.0 copy-start
  0.0 0.0 copy-start.1
  0.0 2.0 %hidden_and_packs.1 = (bf16[512,1024]{1,0:T(8,128)(2,1)S(1)}, bf16[288,1024]{1,0:T(8,128)(2,1)S(1)}, bf16[288,1024]{1,0:T(8,128)(2,1)S(1)}, bf16[96,512]{1,0:T(8,128)(2,1)S(1)}) custom-call(s32[4]{0:T(128)} %level_in.1, bf16[512,1024]{1,0:T(8,128)(2,1)} %frames.1, f32[8,2048]{1,0:T(8,128)} %table_in.1, bf16[96,512]{1,0:T(8,128)(2,1)} %context_in.1), custom_call_target="tpu_custom_call" | custom-call | flops 8000000000 | bytes 4000000 | tf_op jit(solution)/shard_map/hidden_and_packs/pallas_call | solution.py:646
  2.0 0.1 collective-permute-start.1
  2.1 4.6 %collective-permute-start = (bf16[288,1024]{1,0:T(8,128)(2,1)S(1)}, bf16[288,1024]{1,0:T(8,128)(2,1)S(1)}, u32[]{:S(2)}, u32[]{:S(2)}) collective-permute-start(bf16[288,1024]{1,0:T(8,128)(2,1)S(1)} %get-tuple-element.19), channel_id=1, source_target_pairs={{1,2},{3,4},{5,6},{7,8},{9,10},{11,12},{13,14},{2,1},{4,3},{6,5},{... | collective-permute-start | bytes 1769480 | tf_op jit(solution)/shard_map/ppermute | solution.py:671
  6.7 0.0 collective-permute-done.1.near
  6.7 0.0 copy-done.2
  6.8 0.0 copy-done
  6.8 0.0 copy-done.1
  6.8 19.5 %local_attention.1 = (bf16[512,1024]{1,0:T(8,128)(2,1)}, f32[256,1024]{1,0:T(8,128)S(1)}, f32[256,1024]{1,0:T(8,128)S(1)}, f32[256,128]{1,0:T(8,128)S(1)}, bf16[...) custom-call(s32[16]{0:T(128)} %band_in.3, ...), custom_call_target="tpu_custom_call" | custom-call | flops 12000000000 | bytes 20000000 | tf_op jit(solution)/shard_map/local_attention/pallas_call | solution.py:683
  26.3 0.0 collective-permute-done.pack
  26.3 9.6 %halo_attention.1 = bf16[512,1024]{1,0:T(8,128)(2,1)} custom-call(s32[16]{0:T(128)} %band_in.3, f32[16]{0:T(128)} %factor_in.3, f32[8]{0:T(128)} %temp_in.3, s32[2,4]{1,0:T(2,128)} %bitcast.2, s32[4]{0:T(128)} %counts_in.3, bf16[288,1024]{1,0:T(8,128)(2,1)S(1)} %collective-permute-done.pack, ...), custom_call_target="tpu_custom_call", output_to_operand_aliasing={{}: (17, {})} | custom-call | flops 5000000000 | bytes 12000000 | tf_op jit(solution)/shard_map/halo_attention/pallas_call | solution.py:725
Async XLA Ops:
  0.0 6.7 %copy-start.2 = (bf16[512,1024]{1,0:T(8,128)(2,1)S(1)}, bf16[512,1024]{1,0:T(8,128)(2,1)}, u32[]{:S(2)}) copy-start(bf16[512,1024]{1,0:T(8,128)(2,1)} %wckv.3) | copy-start | bytes 3145732
  0.0 6.8 %copy-start = (bf16[1024,3072]{1,0:T(8,128)(2,1)S(1)}, bf16[1024,3072]{1,0:T(8,128)(2,1)}, u32[]{:S(2)}) copy-start(bf16[1024,3072]{1,0:T(8,128)(2,1)} %wqkv.3) | copy-start | bytes 18874372
  0.0 6.8 %copy-start.1 = (bf16[1024,512]{1,0:T(8,128)(2,1)S(1)}, bf16[1024,512]{1,0:T(8,128)(2,1)}, u32[]{:S(2)}) copy-start(bf16[1024,512]{1,0:T(8,128)(2,1)} %wcq.1) | copy-start | bytes 3145732
  2.0 4.8 %collective-permute-start.1 = (bf16[288,1024]{1,0:T(8,128)(2,1)S(1)}, bf16[288,1024]{1,0:T(8,128)(2,1)S(1)}, u32[]{:S(2)}, u32[]{:S(2)}) collective-permute-start(bf16[288,1024]{1,0:T(8,128)(2,1)S(1)} %get-tuple-element.21), channel_id=1, source_target_pairs={{0,1},{1,0},{2,3},{3,2},{4,5},{5,4},{6,7},{7,6},{8,9},{9,8},{10,11... | collective-permute-start | bytes 1769480 | tf_op jit(solution)/shard_map/ppermute | solution.py:670
  2.1 24.2 %collective-permute-start = (bf16[288,1024]{1,0:T(8,128)(2,1)S(1)}, bf16[288,1024]{1,0:T(8,128)(2,1)S(1)}, u32[]{:S(2)}, u32[]{:S(2)}) collective-permute-start(bf16[288,1024]{1,0:T(8,128)(2,1)S(1)} %get-tuple-element.19), channel_id=1, source_target_pairs={{1,2},{3,4},{5,6},{7,8},{9,10},{11,12},{13,14},{2,1},{4,3},{6,5},{... | collective-permute-start | bytes 1769480 | tf_op jit(solution)/shard_map/ppermute | solution.py:671

commit v5 on v4

--- a/solution.py
+++ b/solution.py
@@ -412,10 +412,10 @@
     def _():
         items = [cross_item(p, f, False) for p in range(cross_pairs) for f in range(done)]
         items += [self_item(p, f, False) for p in range(pairs) for f in range(done)]
-        staggered(items)
+        staggered(items, 2)
         copies = project_out()
         staggered(
-            [self_item(p, f, False) for p in range(pairs) for f in range(done, blocks)]
+            [self_item(p, f, False) for p in range(pairs) for f in range(done, blocks)], 2
         )
         for copy in copies:
             copy.wait()
@@ -486,7 +486,7 @@
         (band_in, factor_in, temp_in, align_in, counts_in),
         (band, factor, temp, align, counts),
         sems,
-        WMAX,
+        0,
     )
     vext[:, :, LANES:] = jnp.ones((vext.shape[0], vext.shape[1], LANES), BF16)
     ck[...] = ck_in[...]
@@ -596,7 +596,7 @@
             cross_item(p, f, False) for p in range(cross_pairs) for f in range(done, blocks)
         ]
         items += [self_item(p, f, False) for p in range(pairs) for f in range(done, blocks)]
-        staggered(items, 2)
+        staggered(items, 3)
 
     @pl.when(jnp.logical_not(easy))
     def _():
@@ -608,8 +608,22 @@
         def _(p):
             staggered([cross_item(p, f, True) for f in range(done, blocks)])
 
-    total = dot(mine[...], wo[...]) + dot(cross_mine[...], wco[...])
-    for copy in finish(total, out, stage, sems, done, WMAX, odd, blocks):
+    copies = []
+    for start in range(0, wo.shape[1], CHUNK):
+        cols = slice(start, start + CHUNK)
+        total = dot(mine[...], wo[:, cols]) + dot(cross_mine[...], wco[:, cols])
+        stage[:, cols] = total.astype(BF16)
+        for i in range(WMAX):
+            to = pl.multiple_of(local_block(done + i, odd, blocks) * BLK, BLK)
+            copies.append(
+                pltpu.make_async_copy(
+                    stage.at[pl.ds(i * BLK, BLK), pl.ds(start, CHUNK)],
+                    out.at[pl.ds(to, BLK), pl.ds(start, CHUNK)],
+                    sems.at[len(copies)],
+                )
+            )
+            copies[-1].start()
+    for copy in copies:
         copy.wait()
 
 
@@ -737,7 +751,7 @@
             pltpu.VMEM((open_rows, qwidth), BF16),
             pltpu.VMEM((open_rows, cqwidth), BF16),
             pltpu.VMEM((open_rows, width), BF16),
-            pltpu.SemaphoreType.DMA((WMAX + 5,)),
+            pltpu.SemaphoreType.DMA((max(5, WMAX * width // CHUNK),)),
         ],
         input_output_aliases={17: 0},
         compiler_params=pltpu.CompilerParams(vmem_limit_bytes=TAIL_VMEM),

time: 36.2 us -> 36.1 us (level)
  no operation moved by 1% of the time
where the time goes in v5:
time: 36.1 us; the launch traced here: 36 us
  Pallas kernels  31 us (86%)
  starting transfers between devices  4.75 us (13%)
    pallas_call x1, Pallas kernels, shards(): pl.pallas_call(main_kernel, out_shape=[jax.ShapeDtypeStruct((rows, width)...  19.5 us
    pallas_call x1, Pallas kernels, shards(): pl.pallas_call(tail_kernel, out_shape=jax.ShapeDtypeStruct((rows, width),...  9.51 us
    ppermute x1, starting transfers between devices, shards(): far_got = lax.ppermute(far, 'seq', across)  4.63 us
    pallas_call x1, Pallas kernels, shards(): pl.pallas_call(hidden_kernel, out_shape=[jax.ShapeDtypeStruct((rows, widt...  1.96 us
  transfers between devices with their start and end apart: 2, of which 0 were waited for; matrix products, arithmetic and copies ran while one was open for 0% of the time, Pallas kernels for 54%

profile of v5, /device:TPU:1, one launch (start us, length us, event | category | flops | bytes accessed | tf_op | source)
XLA Modules:
  0.0 36.0 jit_solution(5319550089597772443)
XLA Ops:
  0.0 0.0 copy-start.2
  0.0 0.0 copy-start
  0.0 0.0 copy-start.1
  0.0 2.0 %hidden_and_packs.1 = (bf16[512,1024]{1,0:T(8,128)(2,1)S(1)}, bf16[288,1024]{1,0:T(8,128)(2,1)S(1)}, bf16[288,1024]{1,0:T(8,128)(2,1)S(1)}, bf16[96,512]{1,0:T(8,128)(2,1)S(1)}) custom-call(s32[4]{0:T(128)} %level_in.1, bf16[512,1024]{1,0:T(8,128)(2,1)} %frames.1, f32[8,2048]{1,0:T(8,128)} %table_in.1, bf16[96,512]{1,0:T(8,128)(2,1)} %context_in.1), custom_call_target="tpu_custom_call" | custom-call | flops 8000000000 | bytes 4000000 | tf_op jit(solution)/shard_map/hidden_and_packs/pallas_call | solution.py:660
  2.0 0.1 collective-permute-start.1
  2.1 4.6 %collective-permute-start = (bf16[288,1024]{1,0:T(8,128)(2,1)S(1)}, bf16[288,1024]{1,0:T(8,128)(2,1)S(1)}, u32[]{:S(2)}, u32[]{:S(2)}) collective-permute-start(bf16[288,1024]{1,0:T(8,128)(2,1)S(1)} %get-tuple-element.19), channel_id=1, source_target_pairs={{1,2},{3,4},{5,6},{7,8},{9,10},{11,12},{13,14},{2,1},{4,3},{6,5},{... | collective-permute-start | bytes 1769480 | tf_op jit(solution)/shard_map/ppermute | solution.py:685
  6.7 0.0 collective-permute-done.1.near
  6.7 0.0 copy-done.2
  6.8 0.0 copy-done
  6.8 0.0 copy-done.1
  6.8 19.5 %local_attention.1 = (bf16[512,1024]{1,0:T(8,128)(2,1)}, f32[256,1024]{1,0:T(8,128)S(1)}, f32[256,1024]{1,0:T(8,128)S(1)}, f32[256,128]{1,0:T(8,128)S(1)}, bf16[...) custom-call(s32[16]{0:T(128)} %band_in.3, ...), custom_call_target="tpu_custom_call" | custom-call | flops 12000000000 | bytes 20000000 | tf_op jit(solution)/shard_map/local_attention/pallas_call | solution.py:697
  26.3 0.0 collective-permute-done.pack
  26.3 9.5 %halo_attention.1 = bf16[512,1024]{1,0:T(8,128)(2,1)} custom-call(s32[16]{0:T(128)} %band_in.3, f32[16]{0:T(128)} %factor_in.3, f32[8]{0:T(128)} %temp_in.3, s32[2,4]{1,0:T(2,128)} %bitcast.2, s32[4]{0:T(128)} %counts_in.3, bf16[288,1024]{1,0:T(8,128)(2,1)S(1)} %collective-permute-done.pack, ...), custom_call_target="tpu_custom_call", output_to_operand_aliasing={{}: (17, {})} | custom-call | flops 5000000000 | bytes 12000000 | tf_op jit(solution)/shard_map/halo_attention/pallas_call | solution.py:739
Async XLA Ops:
  0.0 6.7 %copy-start.2 = (bf16[512,1024]{1,0:T(8,128)(2,1)S(1)}, bf16[512,1024]{1,0:T(8,128)(2,1)}, u32[]{:S(2)}) copy-start(bf16[512,1024]{1,0:T(8,128)(2,1)} %wckv.3) | copy-start | bytes 3145732
  0.0 6.8 %copy-start = (bf16[1024,3072]{1,0:T(8,128)(2,1)S(1)}, bf16[1024,3072]{1,0:T(8,128)(2,1)}, u32[]{:S(2)}) copy-start(bf16[1024,3072]{1,0:T(8,128)(2,1)} %wqkv.3) | copy-start | bytes 18874372
  0.0 6.8 %copy-start.1 = (bf16[1024,512]{1,0:T(8,128)(2,1)S(1)}, bf16[1024,512]{1,0:T(8,128)(2,1)}, u32[]{:S(2)}) copy-start(bf16[1024,512]{1,0:T(8,128)(2,1)} %wcq.1) | copy-start | bytes 3145732
  2.0 4.8 %collective-permute-start.1 = (bf16[288,1024]{1,0:T(8,128)(2,1)S(1)}, bf16[288,1024]{1,0:T(8,128)(2,1)S(1)}, u32[]{:S(2)}, u32[]{:S(2)}) collective-permute-start(bf16[288,1024]{1,0:T(8,128)(2,1)S(1)} %get-tuple-element.21), channel_id=1, source_target_pairs={{0,1},{1,0},{2,3},{3,2},{4,5},{5,4},{6,7},{7,6},{8,9},{9,8},{10,11... | collective-permute-start | bytes 1769480 | tf_op jit(solution)/shard_map/ppermute | solution.py:684
  2.1 24.2 %collective-permute-start = (bf16[288,1024]{1,0:T(8,128)(2,1)S(1)}, bf16[288,1024]{1,0:T(8,128)(2,1)S(1)}, u32[]{:S(2)}, u32[]{:S(2)}) collective-permute-start(bf16[288,1024]{1,0:T(8,128)(2,1)S(1)} %get-tuple-element.19), channel_id=1, source_target_pairs={{1,2},{3,4},{5,6},{7,8},{9,10},{11,12},{13,14},{2,1},{4,3},{6,5},{... | collective-permute-start | bytes 1769480 | tf_op jit(solution)/shard_map/ppermute | solution.py:685

commit v6 on v5

--- a/solution.py
+++ b/solution.py
@@ -412,11 +412,10 @@
     def _():
         items = [cross_item(p, f, False) for p in range(cross_pairs) for f in range(done)]
         items += [self_item(p, f, False) for p in range(pairs) for f in range(done)]
+        later = [self_item(p, f, False) for p in range(pairs) for f in range(done, blocks)]
+        copies = []
+        items += later[:2] + [(project_out, copies.extend)] + later[2:]
         staggered(items, 2)
-        copies = project_out()
-        staggered(
-            [self_item(p, f, False) for p in range(pairs) for f in range(done, blocks)], 2
-        )
         for copy in copies:
             copy.wait()
 

time: 36.1 us -> 36.1 us (level)
  no operation moved by 1% of the time
where the time goes in v6:
time: 36.1 us; the launch traced here: 36 us
  Pallas kernels  31 us (86%)
  starting transfers between devices  4.75 us (13%)
    pallas_call x1, Pallas kernels, shards(): pl.pallas_call(main_kernel, out_shape=[jax.ShapeDtypeStruct((rows, width)...  19.5 us
    pallas_call x1, Pallas kernels, shards(): pl.pallas_call(tail_kernel, out_shape=jax.ShapeDtypeStruct((rows, width),...  9.51 us
    ppermute x1, starting transfers between devices, shards(): far_got = lax.ppermute(far, 'seq', across)  4.63 us
    pallas_call x1, Pallas kernels, shards(): pl.pallas_call(hidden_kernel, out_shape=[jax.ShapeDtypeStruct((rows, widt...  1.96 us
  transfers between devices with their start and end apart: 2, of which 0 were waited for; matrix products, arithmetic and copies ran while one was open for 0% of the time, Pallas kernels for 54%

profile of v6, /device:TPU:1, one launch (start us, length us, event | category | flops | bytes accessed | tf_op | source)
XLA Modules:
  0.0 36.0 jit_solution(713181461250821105)
XLA Ops:
  0.0 0.0 copy-start.2
  0.0 0.0 copy-start
  0.0 0.0 copy-start.1
  0.0 2.0 %hidden_and_packs.1 = (bf16[512,1024]{1,0:T(8,128)(2,1)S(1)}, bf16[288,1024]{1,0:T(8,128)(2,1)S(1)}, bf16[288,1024]{1,0:T(8,128)(2,1)S(1)}, bf16[96,512]{1,0:T(8,128)(2,1)S(1)}) custom-call(s32[4]{0:T(128)} %level_in.1, bf16[512,1024]{1,0:T(8,128)(2,1)} %frames.1, f32[8,2048]{1,0:T(8,128)} %table_in.1, bf16[96,512]{1,0:T(8,128)(2,1)} %context_in.1), custom_call_target="tpu_custom_call" | custom-call | flops 8000000000 | bytes 4000000 | tf_op jit(solution)/shard_map/hidden_and_packs/pallas_call | solution.py:659
  2.0 0.1 collective-permute-start.1
  2.1 4.6 %collective-permute-start = (bf16[288,1024]{1,0:T(8,128)(2,1)S(1)}, bf16[288,1024]{1,0:T(8,128)(2,1)S(1)}, u32[]{:S(2)}, u32[]{:S(2)}) collective-permute-start(bf16[288,1024]{1,0:T(8,128)(2,1)S(1)} %get-tuple-element.19), channel_id=1, source_target_pairs={{1,2},{3,4},{5,6},{7,8},{9,10},{11,12},{13,14},{2,1},{4,3},{6,5},{... | collective-permute-start | bytes 1769480 | tf_op jit(solution)/shard_map/ppermute | solution.py:684
  6.7 0.0 collective-permute-done.1.near
  6.7 0.0 copy-done.2
  6.8 0.0 copy-done
  6.8 0.0 copy-done.1
  6.8 19.5 %local_attention.1 = (bf16[512,1024]{1,0:T(8,128)(2,1)}, f32[256,1024]{1,0:T(8,128)S(1)}, f32[256,1024]{1,0:T(8,128)S(1)}, f32[256,128]{1,0:T(8,128)S(1)}, bf16[...) custom-call(s32[16]{0:T(128)} %band_in.3, ...), custom_call_target="tpu_custom_call" | custom-call | flops 12000000000 | bytes 20000000 | tf_op jit(solution)/shard_map/local_attention/pallas_call | solution.py:696
  26.3 0.0 collective-permute-done.pack
  26.3 9.5 %halo_attention.1 = bf16[512,1024]{1,0:T(8,128)(2,1)} custom-call(s32[16]{0:T(128)} %band_in.3, f32[16]{0:T(128)} %factor_in.3, f32[8]{0:T(128)} %temp_in.3, s32[2,4]{1,0:T(2,128)} %bitcast.2, s32[4]{0:T(128)} %counts_in.3, bf16[288,1024]{1,0:T(8,128)(2,1)S(1)} %collective-permute-done.pack, ...), custom_call_target="tpu_custom_call", output_to_operand_aliasing={{}: (17, {})} | custom-call | flops 5000000000 | bytes 12000000 | tf_op jit(solution)/shard_map/halo_attention/pallas_call | solution.py:738
Async XLA Ops:
  0.0 6.7 %copy-start.2 = (bf16[512,1024]{1,0:T(8,128)(2,1)S(1)}, bf16[512,1024]{1,0:T(8,128)(2,1)}, u32[]{:S(2)}) copy-start(bf16[512,1024]{1,0:T(8,128)(2,1)} %wckv.3) | copy-start | bytes 3145732
  0.0 6.8 %copy-start = (bf16[1024,3072]{1,0:T(8,128)(2,1)S(1)}, bf16[1024,3072]{1,0:T(8,128)(2,1)}, u32[]{:S(2)}) copy-start(bf16[1024,3072]{1,0:T(8,128)(2,1)} %wqkv.3) | copy-start | bytes 18874372
  0.0 6.8 %copy-start.1 = (bf16[1024,512]{1,0:T(8,128)(2,1)S(1)}, bf16[1024,512]{1,0:T(8,128)(2,1)}, u32[]{:S(2)}) copy-start(bf16[1024,512]{1,0:T(8,128)(2,1)} %wcq.1) | copy-start | bytes 3145732
  2.0 4.8 %collective-permute-start.1 = (bf16[288,1024]{1,0:T(8,128)(2,1)S(1)}, bf16[288,1024]{1,0:T(8,128)(2,1)S(1)}, u32[]{:S(2)}, u32[]{:S(2)}) collective-permute-start(bf16[288,1024]{1,0:T(8,128)(2,1)S(1)} %get-tuple-element.21), channel_id=1, source_target_pairs={{0,1},{1,0},{2,3},{3,2},{4,5},{5,4},{6,7},{7,6},{8,9},{9,8},{10,11... | collective-permute-start | bytes 1769480 | tf_op jit(solution)/shard_map/ppermute | solution.py:683
  2.1 24.2 %collective-permute-start = (bf16[288,1024]{1,0:T(8,128)(2,1)S(1)}, bf16[288,1024]{1,0:T(8,128)(2,1)S(1)}, u32[]{:S(2)}, u32[]{:S(2)}) collective-permute-start(bf16[288,1024]{1,0:T(8,128)(2,1)S(1)} %get-tuple-element.19), channel_id=1, source_target_pairs={{1,2},{3,4},{5,6},{7,8},{9,10},{11,12},{13,14},{2,1},{4,3},{6,5},{... | collective-permute-start | bytes 1769480 | tf_op jit(solution)/shard_map/ppermute | solution.py:684
